TPU v7x, 128 devices: a whole 4x4x4 slice. The times are simulated.
128 devices in a mesh: lat: 8 (over y, z_hi), lon: 16 (over x, z_lo, core).
Axes of the slice: x: 4, y: 4, z: 4 (z_hi: 2, z_lo: 2; z = z_hi * 2 + z_lo), core: 2. Of those that a mesh axis runs over, the one named last changes fastest.
Arguments:
- coarse: bfloat16 [73, 32, 128], P(None, 'lat', 'lon'), may hold values from -6 to 6
- row_src: int32 [256], P('lat'), may hold values from 0 to 30, as said below
- row_frac: float32 [256], P('lat'), may hold values from 0 to 1
- col_src: int32 [2048], P('lon'), may hold values from 0 to 127, as said below
- col_frac: float32 [2048], P('lon'), may hold values from 0 to 1
- embed_weight: bfloat16 [73, 128], replicated, may hold values from -0.75 to 0.75
- conv1_weight: bfloat16 [3, 3, 128, 128], replicated, may hold values from -0.1875 to 0.1875
- conv2_weight: bfloat16 [3, 3, 128, 128], replicated, may hold values from -0.1875 to 0.1875
- cotangent: bfloat16 [256, 2048, 128], P('lat', 'lon'), may hold values from -6 to 6
Outputs:
- features: bfloat16 [256, 2048, 128], P('lat', 'lon')
- grad_embed: float32 [73, 128], replicated
- grad_conv1: float32 [3, 3, 128, 128], replicated
- grad_conv2: float32 [3, 3, 128, 128], replicated
Inputs may be any that keep to these rules, and one draw needn't show every extreme that they name: row_src[r] differs from (r * 32) // 256 by at most 1; both bounds are reached. col_src[c] differs cyclically (mod 128) from (c * 128) // 2048 by at most 1; both bounds are reached.
All inputs are finite; a program needn't handle non-finite values.
Results may differ from a plain program's by a relative error of at most 0.0062.
Values may be sent and summed in bfloat16 or wider, within the bound.
A program may use at most 128 MiB of HBM per device.

v0:
```python
import math

import jax
import jax.numpy as jnp
from jax import lax
from jax.sharding import PartitionSpec as P


def with_halo(x, sides, width):
    for axis, dim in sides:
        peers, length = (lax.axis_size(axis), x.shape[dim])
        up = [(i, (i + 1) % peers) for i in range(peers)]
        down = [(j, i) for i, j in up]
        last = lax.slice_in_dim(x, length - width, length, axis=dim)
        first = lax.slice_in_dim(x, 0, width, axis=dim)
        before = lax.ppermute(last, axis, up)
        after = lax.ppermute(first, axis, down)
        x = jnp.concatenate([before, x, after], axis=dim)
    return x


def edge_zero(padded, depth, lat_place, lat_count):
    line = jnp.arange(padded.shape[0])
    keep = ((line >= depth) | (lat_place > 0)) & (
        (line < padded.shape[0] - depth) | (lat_place < lat_count - 1)
    )
    return padded * keep.astype(padded.dtype)[:, None, None]


def convolve(padded, weight, span_rows, span_cols):
    channels = weight.shape[2]
    total = jnp.zeros((span_rows * span_cols, weight.shape[3]), jnp.float32)
    for tap_row in range(3):
        for tap_col in range(3):
            window = padded[tap_row : tap_row + span_rows, tap_col : tap_col + span_cols].reshape(
                -1, channels
            )
            total = total + jnp.dot(
                window, weight[tap_row, tap_col], preferred_element_type=jnp.float32
            )
    return total.reshape(span_rows, span_cols, -1)


def convolve_back(padded, weight, span_rows, span_cols):
    channels = weight.shape[3]
    total = jnp.zeros((span_rows * span_cols, weight.shape[2]), jnp.float32)
    for tap_row in range(3):
        for tap_col in range(3):
            window = padded[
                2 - tap_row : 2 - tap_row + span_rows, 2 - tap_col : 2 - tap_col + span_cols
            ].reshape(-1, channels)
            total = total + jnp.dot(
                window, weight[tap_row, tap_col].T, preferred_element_type=jnp.float32
            )
    return total.reshape(span_rows, span_cols, -1)


def weight_grads(padded, delta, span_rows, span_cols):
    channels = padded.shape[2]
    flat_delta = delta.reshape(-1, delta.shape[2])
    blocks = []
    for tap_row in range(3):
        line = []
        for tap_col in range(3):
            window = padded[tap_row : tap_row + span_rows, tap_col : tap_col + span_cols].reshape(
                -1, channels
            )
            line.append(
                lax.dot_general(
                    window, flat_delta, (((0,), (0,)), ((), ())), preferred_element_type=jnp.float32
                )
            )
        blocks.append(jnp.stack(line))
    return jnp.stack(blocks)


def blend_matrix(local_index, fraction, length):
    line = jnp.arange(length, dtype=jnp.int32)
    lower = (line[None, :] == local_index[:, None]).astype(jnp.float32)
    upper = (line[None, :] == local_index[:, None] + 1).astype(jnp.float32)
    return (1.0 - fraction)[:, None] * lower + fraction[:, None] * upper


def lift_cells(
    widened,
    row_index,
    row_weight,
    col_index,
    col_weight,
    embed_weight,
    lat_place,
    lon_place,
    band_rows,
    band_cols,
    lon_count,
):
    row_local = row_index - (lat_place * band_rows - 3)
    col_local = jnp.mod(col_index - lon_place * band_cols + 3, band_cols * lon_count)
    row_blend = blend_matrix(row_local, row_weight, band_rows + 6)
    col_blend = blend_matrix(col_local, col_weight, band_cols + 6)
    row_mixed = jnp.einsum("rj,kjl->krl", row_blend, widened, precision=lax.Precision.HIGHEST)
    fine_input = jnp.einsum(
        "krl,cl->krc", row_mixed, col_blend, precision=lax.Precision.HIGHEST
    ).astype(jnp.bfloat16)
    lifted = jnp.einsum(
        "krc,kh->rch", fine_input, embed_weight, preferred_element_type=jnp.float32
    ).astype(jnp.bfloat16)
    return (fine_input, lifted)


def on_device(
    coarse,
    row_src,
    row_frac,
    col_src,
    col_frac,
    embed_weight,
    conv1_weight,
    conv2_weight,
    cotangent,
):
    lat_count = lax.axis_size("lat")
    lon_count = lax.axis_size("lon")
    lat_place = lax.axis_index("lat")
    lon_place = lax.axis_index("lon")
    band_rows = coarse.shape[1]
    band_cols = coarse.shape[2]
    tile_rows = cotangent.shape[0]
    tile_cols = cotangent.shape[1]
    widened = with_halo(coarse, (("lat", 1), ("lon", 2)), 3).astype(jnp.float32)
    fine_input, lifted = lift_cells(
        widened,
        row_src,
        row_frac,
        col_src,
        col_frac,
        embed_weight,
        lat_place,
        lon_place,
        band_rows,
        band_cols,
        lon_count,
    )
    lifted_pad = edge_zero(with_halo(lifted, (("lat", 0), ("lon", 1)), 1), 1, lat_place, lat_count)
    pre_first = convolve(lifted_pad, conv1_weight, tile_rows, tile_cols)
    hidden = jax.nn.silu(pre_first).astype(jnp.bfloat16)
    hidden_pad = edge_zero(with_halo(hidden, (("lat", 0), ("lon", 1)), 1), 1, lat_place, lat_count)
    features = (
        lifted.astype(jnp.float32) + convolve(hidden_pad, conv2_weight, tile_rows, tile_cols)
    ).astype(jnp.bfloat16)
    cot_pad = edge_zero(with_halo(cotangent, (("lat", 0), ("lon", 1)), 1), 1, lat_place, lat_count)
    grad_second = weight_grads(hidden_pad, cotangent, tile_rows, tile_cols)
    back_hidden = convolve_back(cot_pad, conv2_weight, tile_rows, tile_cols)
    sig = jax.nn.sigmoid(pre_first)
    delta = (back_hidden * sig * (1.0 + pre_first * (1.0 - sig))).astype(jnp.bfloat16)
    delta_pad = edge_zero(with_halo(delta, (("lat", 0), ("lon", 1)), 1), 1, lat_place, lat_count)
    grad_first = weight_grads(lifted_pad, delta, tile_rows, tile_cols)
    back_lifted = (
        cotangent.astype(jnp.float32) + convolve_back(delta_pad, conv1_weight, tile_rows, tile_cols)
    ).astype(jnp.bfloat16)
    grad_lift = jnp.einsum(
        "krc,rch->kh", fine_input, back_lifted, preferred_element_type=jnp.float32
    )
    norm_scale = 1.0 / math.sqrt(tile_rows * lat_count * tile_cols * lon_count)
    terms = (grad_lift * norm_scale, grad_first * norm_scale, grad_second * norm_scale)
    totals = lax.psum((terms[0], terms[1], terms[2]), ("lat", "lon"))
    return (features, totals[0], totals[1], totals[2])


def solution(mesh):
    in_specs = (
        P(None, "lat", "lon"),
        P("lat"),
        P("lat"),
        P("lon"),
        P("lon"),
        P(),
        P(),
        P(),
        P("lat", "lon", None),
    )
    out_specs = (P("lat", "lon", None), P(), P(), P())
    return jax.shard_map(
        on_device, mesh=mesh, in_specs=in_specs, out_specs=out_specs, check_vma=False
    )
```

profile of v0, /device:TPU:1, one launch (start us, length us, event | category | flops | bytes accessed | tf_op | source)
XLA Modules:
  0.0 357.9 jit_solution(3271548695085398036)
XLA Ops:
  7.2 0.8 fusion.132
  8.0 6.9 %collective-permute-start.1 = (bf16[73,3,8]{0,2,1:T(8,128)(2,1)S(1)}, bf16[73,3,8]{0,2,1:T(8,128)(2,1)S(1)}, u32[]{:S(2)}, u32[]{:S(2)}) collective-permute-start(bf16[73,3,8]{0,2,1:T(8,128)(2,1)S(1)} %get-tuple-element.66), channel_id=1, source_target_pairs={{16,0},{32,16},{48,32},{64,48},{80,64},{96,80},{112,96},{0,112},{1... | collective-permute-start | bytes 10520 | tf_op jit(solution)/shard_map/ppermute | solution.py:17
  14.9 0.8 fusion.128
  15.7 5.1 %collective-permute-start.13 = (bf16[1,128,128]{2,1,0:T(8,128)(2,1)S(1)}, bf16[1,128,128]{2,1,0:T(8,128)(2,1)S(1)}, u32[]{:S(2)}, u32[]{:S(2)}) collective-permute-start(bf16[1,128,128]{2,1,0:T(8,128)(2,1)S(1)} %get-tuple-element.58), channel_id=1, source_target_pairs={{16,0},{32,16},{48,32},{64,48},{80,64},{96,80},{112,96},{0,112},{1... | collective-permute-start | bytes 98312 | tf_op jit(solution)/shard_map/ppermute | solution.py:17
  20.7 0.7 broadcast_add_fusion.1
  21.4 0.7 broadcast_add_fusion
  22.7 0.7 constant_dynamic-update-slice_fusion.1
  23.5 2.2 collective-permute-start.2
  25.7 0.7 broadcast_subtract_fusion
  26.5 2.6 collective-permute-done.3
  29.1 1.1 fusion.4
  30.5 2.7 convolution_convert_fusion.1
  33.8 1.2 collective-permute-start.4
  34.9 5.0 %collective-permute-start.5 = (bf16[1,128,128]{2,1,0:T(8,128)(2,1)S(1)}, bf16[1,128,128]{2,1,0:T(8,128)(2,1)S(1)}, u32[]{:S(2)}, u32[]{:S(2)}) collective-permute-start(bf16[1,128,128]{2,1,0:T(8,128)(2,1)S(1)} %get-tuple-element.63), channel_id=1, source_target_pairs={{16,0},{32,16},{48,32},{64,48},{80,64},{96,80},{112,96},{0,112},{1... | collective-permute-start | bytes 98312 | tf_op jit(solution)/shard_map/ppermute | solution.py:17
  40.2 1.0 collective-permute-start.15
  41.2 0.9 collective-permute-start.6
  42.1 3.0 collective-permute-start.7
  46.0 1.9 maximum_multiply_fusion.2
  47.9 5.9 %fusion.123 = (bf16[32,128,128]{2,1,0:T(8,128)(2,1)}, bf16[32,128,128]{2,1,0:T(8,128)(2,1)}, bf16[32,128,128]{2,1,0:T(8,128)(2,1)S(1)}, bf16[32,128,128]{2,1,0:T...) fusion(bf16[34,130,128]{2,1,0:T(8,128)(2,1)S(1)} %get-tuple-ele, ...), kind=kLoop, calls=%fused_computation.222 | loop fusion | bytes 37748736 | tf_op jit(solution)/shard_map/slice | solution.py:49
  53.8 1.7 fusion.22
  56.0 0.8 copy-done.18
  57.3 0.8 copy-done.17
  58.5 0.8 copy-done.16
  60.6 0.8 copy-done.15
  61.8 0.8 copy-done.14
  63.1 0.8 copy-done.13
  64.8 0.8 copy-done.11
  68.6 1.0 multiply_convert_fusion
  74.1 5.1 %collective-permute-start.9 = (bf16[1,128,128]{2,1,0:T(8,128)(2,1)S(1)}, bf16[1,128,128]{2,1,0:T(8,128)(2,1)S(1)}, u32[]{:S(2)}, u32[]{:S(2)}) collective-permute-start(bf16[1,128,128]{2,1,0:T(8,128)(2,1)S(1)} %get-tuple-element.61), channel_id=1, source_target_pairs={{16,0},{32,16},{48,32},{64,48},{80,64},{96,80},{112,96},{0,112},{1... | collective-permute-start | bytes 98312 | tf_op jit(solution)/shard_map/ppermute | solution.py:17
  79.1 9.4 %collective-permute-start.16 = (bf16[1,128,128]{2,1,0:T(8,128)(2,1)S(1)}, bf16[1,128,128]{2,1,0:T(8,128)(2,1)S(1)}, u32[]{:S(2)}, u32[]{:S(2)}) collective-permute-start(bf16[1,128,128]{2,1,0:T(8,128)(2,1)S(1)} %get-tuple-element.56), channel_id=1, source_target_pairs={{0,16},{16,32},{32,48},{48,64},{64,80},{80,96},{96,112},{112,0},{1... | collective-permute-start | bytes 98312 | tf_op jit(solution)/shard_map/ppermute | solution.py:16
  88.6 5.1 %collective-permute-start.17 = (bf16[1,128,128]{2,1,0:T(8,128)(2,1)S(1)}, bf16[1,128,128]{2,1,0:T(8,128)(2,1)S(1)}, u32[]{:S(2)}, u32[]{:S(2)}) collective-permute-start(bf16[1,128,128]{2,1,0:T(8,128)(2,1)S(1)} %get-tuple-element.57), channel_id=1, source_target_pairs={{16,0},{32,16},{48,32},{64,48},{80,64},{96,80},{112,96},{0,112},{1... | collective-permute-start | bytes 98312 | tf_op jit(solution)/shard_map/ppermute | solution.py:17
  93.8 1.2 collective-permute-start.10
  95.0 4.5 %collective-permute-start.11 = (bf16[34,1,128]{2,1,0:T(2,128)(2,1)S(1)}, bf16[34,1,128]{2,1,0:T(2,128)(2,1)S(1)}, u32[]{:S(2)}, u32[]{:S(2)}) collective-permute-start(bf16[34,1,128]{2,1,0:T(2,128)(2,1)S(1)} %get-tuple-element.53), channel_id=1, source_target_pairs={{1,0},{2,1},{3,2},{4,3},{5,4},{6,5},{7,6},{8,7},{9,8},{10,9},{11,1... | collective-permute-start | bytes 26120 | tf_op jit(solution)/shard_map/ppermute | solution.py:17
  99.6 3.8 %collective-permute-start.19 = (bf16[34,1,128]{2,1,0:T(2,128)(2,1)S(1)}, bf16[34,1,128]{2,1,0:T(2,128)(2,1)S(1)}, u32[]{:S(2)}, u32[]{:S(2)}) collective-permute-start(bf16[34,1,128]{2,1,0:T(2,128)(2,1)S(1)} %get-tuple-element.49), channel_id=1, source_target_pairs={{1,0},{2,1},{3,2},{4,3},{5,4},{6,5},{7,6},{8,7},{9,8},{10,9},{11,1... | collective-permute-start | bytes 26120 | tf_op jit(solution)/shard_map/ppermute | solution.py:17
  103.4 0.9 maximum_multiply_fusion.4
  104.3 2.5 maximum_multiply_fusion.3
  106.8 1.1 convolution_bitcast_fusion
  107.9 1.1 convolution_bitcast_fusion.8
  109.1 1.1 convolution_bitcast_fusion.7
  110.2 1.1 convolution_bitcast_fusion.6
  111.3 1.1 convolution_bitcast_fusion.5
  112.4 1.1 convolution_bitcast_fusion.4
  113.5 1.1 convolution_bitcast_fusion.3
  114.6 1.1 convolution_bitcast_fusion.2
  115.7 1.1 convolution_bitcast_fusion.1
  116.8 3.8 %fusion.124 = (bf16[32,128,128]{2,1,0:T(8,128)(2,1)}, bf16[32,128,128]{2,1,0:T(8,128)(2,1)}, bf16[32,128,128]{2,1,0:T(8,128)(2,1)}, bf16[32,128,128]{2,1,0:T(8,1...) fusion(bf16[34,130,128]{2,1,0:T(8,128)(2,1)S(1)} %get-tuple-ele, ...), kind=kLoop, calls=%fused_computation.223 | loop fusion | bytes 18874368 | tf_op jit(solution)/shard_map/slice | solution.py:35
  121.1 2.1 fusion.122
  127.1 0.8 copy-done.3
  128.3 69.8 %psum.21 = f32[73,128]{1,0:T(8,128)} all-reduce(f32[73,128]{1,0:T(8,128)S(1)} %fusion), channel_id=1, replica_groups=mesh['lat'=8,'lon'=16] {'lat','lon'}, use_global_device_ids=true, to_apply=%region_0.1 | all-reduce | flops 9344 | bytes 74752 | tf_op jit(solution)/shard_map/psum | solution.py:166
  198.1 0.9 maximum_bitcast_fusion.3
  199.0 0.9 maximum_bitcast_fusion.4
  200.0 0.9 maximum_bitcast_fusion.5
  200.9 0.9 maximum_multiply_fusion.5
  201.8 1.7 convolution_add_fusion.23
  203.9 0.8 copy-done.9
  205.2 0.8 copy-done.8
  206.4 0.8 copy-done.7
  207.6 0.8 copy-done.6
  208.9 0.8 copy-done.5
  210.1 0.8 copy-done.4
  211.3 1.3 add_convert_fusion.1
  212.6 134.3 %all-reduce.3.cloned.1.call-done = (f32[3,3,128,128]{3,2,1,0:T(8,128)}, f32[3,3,128,128]{3,2,1,0:T(8,128)}) async-done(((f32[3,3,128,128]{3,2,1,0:T(8,128)}, f32[3,3,128,128]{3,2,1,0:T(8,128)}), (f32[3,3,128,128]{3,2,1,0:T(8,128)}, f32[3,3,128,128]{3,2,1,0:T(8,128)})) %all-reduce.3.cloned.1.call-update) | async-done | bytes 1179664 | tf_op jit(solution)/shard_map/psum | solution.py:166
  347.0 1.9 copy.65
  348.9 1.9 copy.66
  (122 shorter events, 22.7 us)
Async XLA Ops:
  7.2 26.1 %copy-start = (bf16[73,128]{1,0:T(8,128)(2,1)S(1)}, bf16[73,128]{1,0:T(8,128)(2,1)}, u32[]{:S(2)}) copy-start(bf16[73,128]{1,0:T(8,128)(2,1)} %param.14) | copy-start | bytes 56068
  7.2 339.8 %all-reduce.3.cloned.1.call-start = ((), (), s32[]{:S(2)}) async-start(), calls=%async_computation | async-start | bytes 2359296 | tf_op jit(solution)/shard_map/psum | solution.py:166
  8.0 15.4 %collective-permute-start.1 = (bf16[73,3,8]{0,2,1:T(8,128)(2,1)S(1)}, bf16[73,3,8]{0,2,1:T(8,128)(2,1)S(1)}, u32[]{:S(2)}, u32[]{:S(2)}) collective-permute-start(bf16[73,3,8]{0,2,1:T(8,128)(2,1)S(1)} %get-tuple-element.66), channel_id=1, source_target_pairs={{16,0},{32,16},{48,32},{64,48},{80,64},{96,80},{112,96},{0,112},{1... | collective-permute-start | bytes 10520 | tf_op jit(solution)/shard_map/ppermute | solution.py:17
  14.9 7.8 %collective-permute-start = (bf16[73,3,8]{0,2,1:T(8,128)(2,1)S(1)}, bf16[73,3,8]{0,2,1:T(8,128)(2,1)S(1)}, u32[]{:S(2)}, u32[]{:S(2)}) collective-permute-start(bf16[73,3,8]{0,2,1:T(8,128)(2,1)S(1)} %get-tuple-element.67), channel_id=1, source_target_pairs={{0,16},{16,32},{32,48},{48,64},{64,80},{80,96},{96,112},{112,0},{1... | collective-permute-start | bytes 10520 | tf_op jit(solution)/shard_map/ppermute | solution.py:16
  15.7 24.4 %collective-permute-start.13 = (bf16[1,128,128]{2,1,0:T(8,128)(2,1)S(1)}, bf16[1,128,128]{2,1,0:T(8,128)(2,1)S(1)}, u32[]{:S(2)}, u32[]{:S(2)}) collective-permute-start(bf16[1,128,128]{2,1,0:T(8,128)(2,1)S(1)} %get-tuple-element.58), channel_id=1, source_target_pairs={{16,0},{32,16},{48,32},{64,48},{80,64},{96,80},{112,96},{0,112},{1... | collective-permute-start | bytes 98312 | tf_op jit(solution)/shard_map/ppermute | solution.py:17
  20.7 19.1 %collective-permute-start.12 = (bf16[1,128,128]{2,1,0:T(8,128)(2,1)S(1)}, bf16[1,128,128]{2,1,0:T(8,128)(2,1)S(1)}, u32[]{:S(2)}, u32[]{:S(2)}) collective-permute-start(bf16[1,128,128]{2,1,0:T(8,128)(2,1)S(1)} %get-tuple-element.59), channel_id=1, source_target_pairs={{0,16},{16,32},{32,48},{48,64},{64,80},{80,96},{96,112},{112,0},{1... | collective-permute-start | bytes 98312 | tf_op jit(solution)/shard_map/ppermute | solution.py:16
  23.5 3.0 collective-permute-start.2
  25.7 3.4 collective-permute-start.3
  29.1 10.8 %copy-start.2 = (bf16[32,128,128]{2,1,0:T(8,128)(2,1)S(1)}, bf16[32,128,128]{2,1,0:T(8,128)(2,1)}, u32[]{:S(2)}) copy-start(bf16[32,128,128]{2,1,0:T(8,128)(2,1)} %param.17) | copy-start | bytes 3145732
  33.8 7.4 %collective-permute-start.4 = (bf16[1,128,128]{2,1,0:T(8,128)(2,1)S(1)}, bf16[1,128,128]{2,1,0:T(8,128)(2,1)S(1)}, u32[]{:S(2)}, u32[]{:S(2)}) collective-permute-start(bf16[1,128,128]{2,1,0:T(8,128)(2,1)S(1)} %get-tuple-element.62), channel_id=1, source_target_pairs={{0,16},{16,32},{32,48},{48,64},{64,80},{80,96},{96,112},{112,0},{1... | collective-permute-start | bytes 98312 | tf_op jit(solution)/shard_map/ppermute | solution.py:16
  34.9 6.3 %collective-permute-start.5 = (bf16[1,128,128]{2,1,0:T(8,128)(2,1)S(1)}, bf16[1,128,128]{2,1,0:T(8,128)(2,1)S(1)}, u32[]{:S(2)}, u32[]{:S(2)}) collective-permute-start(bf16[1,128,128]{2,1,0:T(8,128)(2,1)S(1)} %get-tuple-element.63), channel_id=1, source_target_pairs={{16,0},{32,16},{48,32},{64,48},{80,64},{96,80},{112,96},{0,112},{1... | collective-permute-start | bytes 98312 | tf_op jit(solution)/shard_map/ppermute | solution.py:17
  40.1 5.0 %collective-permute-start.14 = (bf16[34,1,128]{2,1,0:T(2,128)(2,1)S(1)}, bf16[34,1,128]{2,1,0:T(2,128)(2,1)S(1)}, u32[]{:S(2)}, u32[]{:S(2)}) collective-permute-start(bf16[34,1,128]{2,1,0:T(2,128)(2,1)S(1)} %get-tuple-element.50), channel_id=1, source_target_pairs={{0,1},{1,2},{2,3},{3,4},{4,5},{5,6},{6,7},{7,8},{8,9},{9,10},{10,1... | collective-permute-start | bytes 26120 | tf_op jit(solution)/shard_map/ppermute | solution.py:16
  40.2 5.0 %collective-permute-start.15 = (bf16[34,1,128]{2,1,0:T(2,128)(2,1)S(1)}, bf16[34,1,128]{2,1,0:T(2,128)(2,1)S(1)}, u32[]{:S(2)}, u32[]{:S(2)}) collective-permute-start(bf16[34,1,128]{2,1,0:T(2,128)(2,1)S(1)} %get-tuple-element.51), channel_id=1, source_target_pairs={{1,0},{2,1},{3,2},{4,3},{5,4},{6,5},{7,6},{8,7},{9,8},{10,9},{11,1... | collective-permute-start | bytes 26120 | tf_op jit(solution)/shard_map/ppermute | solution.py:17
  41.2 4.5 %collective-permute-start.6 = (bf16[34,1,128]{2,1,0:T(2,128)(2,1)S(1)}, bf16[34,1,128]{2,1,0:T(2,128)(2,1)S(1)}, u32[]{:S(2)}, u32[]{:S(2)}) collective-permute-start(bf16[34,1,128]{2,1,0:T(2,128)(2,1)S(1)} %get-tuple-element.54), channel_id=1, source_target_pairs={{0,1},{1,2},{2,3},{3,4},{4,5},{5,6},{6,7},{7,8},{8,9},{9,10},{10,1... | collective-permute-start | bytes 26120 | tf_op jit(solution)/shard_map/ppermute | solution.py:16
  42.1 3.9 %collective-permute-start.7 = (bf16[34,1,128]{2,1,0:T(2,128)(2,1)S(1)}, bf16[34,1,128]{2,1,0:T(2,128)(2,1)S(1)}, u32[]{:S(2)}, u32[]{:S(2)}) collective-permute-start(bf16[34,1,128]{2,1,0:T(2,128)(2,1)S(1)} %get-tuple-element.55), channel_id=1, source_target_pairs={{1,0},{2,1},{3,2},{4,3},{5,4},{6,5},{7,6},{8,7},{9,8},{10,9},{11,1... | collective-permute-start | bytes 26120 | tf_op jit(solution)/shard_map/ppermute | solution.py:17
  47.9 5.9 %copy-start.21 = (bf16[3,3,128,128]{3,2,1,0:T(8,128)(2,1)S(1)}, bf16[3,3,128,128]{3,2,1,0:T(8,128)(2,1)}, u32[]{:S(2)}) copy-start(bf16[3,3,128,128]{3,2,1,0:T(8,128)(2,1)} %param.16) | copy-start | bytes 884740
  53.8 1.8 copy-start.19
  55.6 1.2 copy-start.18
  56.8 1.2 copy-start.17
  58.0 1.2 copy-start.16
  60.1 1.2 copy-start.15
  61.4 1.2 copy-start.14
  62.6 1.2 copy-start.13
  62.6 1.3 copy-start.20
  63.0 1.3 copy-start.12
  64.4 1.2 copy-start.11
  74.0 19.7 %collective-permute-start.8 = (bf16[1,128,128]{2,1,0:T(8,128)(2,1)S(1)}, bf16[1,128,128]{2,1,0:T(8,128)(2,1)S(1)}, u32[]{:S(2)}, u32[]{:S(2)}) collective-permute-start(bf16[1,128,128]{2,1,0:T(8,128)(2,1)S(1)} %get-tuple-element.60), channel_id=1, source_target_pairs={{0,16},{16,32},{32,48},{48,64},{64,80},{80,96},{96,112},{112,0},{1... | collective-permute-start | bytes 98312 | tf_op jit(solution)/shard_map/ppermute | solution.py:16
  74.1 19.7 %collective-permute-start.9 = (bf16[1,128,128]{2,1,0:T(8,128)(2,1)S(1)}, bf16[1,128,128]{2,1,0:T(8,128)(2,1)S(1)}, u32[]{:S(2)}, u32[]{:S(2)}) collective-permute-start(bf16[1,128,128]{2,1,0:T(8,128)(2,1)S(1)} %get-tuple-element.61), channel_id=1, source_target_pairs={{16,0},{32,16},{48,32},{64,48},{80,64},{96,80},{112,96},{0,112},{1... | collective-permute-start | bytes 98312 | tf_op jit(solution)/shard_map/ppermute | solution.py:17
  79.1 20.3 %collective-permute-start.16 = (bf16[1,128,128]{2,1,0:T(8,128)(2,1)S(1)}, bf16[1,128,128]{2,1,0:T(8,128)(2,1)S(1)}, u32[]{:S(2)}, u32[]{:S(2)}) collective-permute-start(bf16[1,128,128]{2,1,0:T(8,128)(2,1)S(1)} %get-tuple-element.56), channel_id=1, source_target_pairs={{0,16},{16,32},{32,48},{48,64},{64,80},{80,96},{96,112},{112,0},{1... | collective-permute-start | bytes 98312 | tf_op jit(solution)/shard_map/ppermute | solution.py:16
  88.6 10.9 %collective-permute-start.17 = (bf16[1,128,128]{2,1,0:T(8,128)(2,1)S(1)}, bf16[1,128,128]{2,1,0:T(8,128)(2,1)S(1)}, u32[]{:S(2)}, u32[]{:S(2)}) collective-permute-start(bf16[1,128,128]{2,1,0:T(8,128)(2,1)S(1)} %get-tuple-element.57), channel_id=1, source_target_pairs={{16,0},{32,16},{48,32},{64,48},{80,64},{96,80},{112,96},{0,112},{1... | collective-permute-start | bytes 98312 | tf_op jit(solution)/shard_map/ppermute | solution.py:17
  93.8 10.5 %collective-permute-start.10 = (bf16[34,1,128]{2,1,0:T(2,128)(2,1)S(1)}, bf16[34,1,128]{2,1,0:T(2,128)(2,1)S(1)}, u32[]{:S(2)}, u32[]{:S(2)}) collective-permute-start(bf16[34,1,128]{2,1,0:T(2,128)(2,1)S(1)} %get-tuple-element.52), channel_id=1, source_target_pairs={{0,1},{1,2},{2,3},{3,4},{4,5},{5,6},{6,7},{7,8},{8,9},{9,10},{10,1... | collective-permute-start | bytes 26120 | tf_op jit(solution)/shard_map/ppermute | solution.py:16
  95.0 9.3 %collective-permute-start.11 = (bf16[34,1,128]{2,1,0:T(2,128)(2,1)S(1)}, bf16[34,1,128]{2,1,0:T(2,128)(2,1)S(1)}, u32[]{:S(2)}, u32[]{:S(2)}) collective-permute-start(bf16[34,1,128]{2,1,0:T(2,128)(2,1)S(1)} %get-tuple-element.53), channel_id=1, source_target_pairs={{1,0},{2,1},{3,2},{4,3},{5,4},{6,5},{7,6},{8,7},{9,8},{10,9},{11,1... | collective-permute-start | bytes 26120 | tf_op jit(solution)/shard_map/ppermute | solution.py:17
  99.5 4.8 %collective-permute-start.18 = (bf16[34,1,128]{2,1,0:T(2,128)(2,1)S(1)}, bf16[34,1,128]{2,1,0:T(2,128)(2,1)S(1)}, u32[]{:S(2)}, u32[]{:S(2)}) collective-permute-start(bf16[34,1,128]{2,1,0:T(2,128)(2,1)S(1)} %get-tuple-element.48), channel_id=1, source_target_pairs={{0,1},{1,2},{2,3},{3,4},{4,5},{5,6},{6,7},{7,8},{8,9},{9,10},{10,1... | collective-permute-start | bytes 26120 | tf_op jit(solution)/shard_map/ppermute | solution.py:16
  99.6 4.7 %collective-permute-start.19 = (bf16[34,1,128]{2,1,0:T(2,128)(2,1)S(1)}, bf16[34,1,128]{2,1,0:T(2,128)(2,1)S(1)}, u32[]{:S(2)}, u32[]{:S(2)}) collective-permute-start(bf16[34,1,128]{2,1,0:T(2,128)(2,1)S(1)} %get-tuple-element.49), channel_id=1, source_target_pairs={{1,0},{2,1},{3,2},{4,3},{5,4},{6,5},{7,6},{8,7},{9,8},{10,9},{11,1... | collective-permute-start | bytes 26120 | tf_op jit(solution)/shard_map/ppermute | solution.py:17
  126.6 1.2 copy-start.3
  201.8 1.7 copy-start.10
  203.5 1.2 copy-start.9
  204.7 1.2 copy-start.8
  206.0 1.2 copy-start.7
  207.2 1.2 copy-start.6
  208.4 1.2 copy-start.5
  209.7 1.2 copy-start.4
  211.3 139.5 %copy-start.1 = (bf16[73,128]{1,0:T(8,128)(2,1)S(1)}, bf16[73,128]{1,0:T(8,128)(2,1)}, u32[]{:S(2)}) copy-start(bf16[73,128]{1,0:T(8,128)(2,1)} %param.14) | copy-start | bytes 56068
Sparse Core Ops, SparseCore 0:
  201.9 145.0 all-reduce.2
where the time goes:
time: 362 us; the launch traced here: 358 us
  waiting for transfers between devices  138 us (38%)
  blocking collectives  69.8 us (19%)
  starting transfers between devices  54.5 us (15%)
  matrix products  37 us (10%)
  local copies, waits for them, and re-layouts  29.7 us (8%)
  between operations  14.9 us (4%)
  other arithmetic  14.1 us (4%)
    psum x1, waiting for transfers between devices, on_device(): totals = lax.psum((terms[0], terms[1], terms[2]), ('lat', 'lon'))  134 us
    psum x1, blocking collectives, on_device(): totals = lax.psum((terms[0], terms[1], terms[2]), ('lat', 'lon'))  69.8 us
    ppermute x10, starting transfers between devices, with_halo(): after = lax.ppermute(first, axis, down)  39.3 us
    unnamed x50, local copies, waits for them, and re-layouts  16 us
    ppermute x10, starting transfers between devices, with_halo(): before = lax.ppermute(last, axis, up)  15.2 us
    dot_general x18, matrix products, weight_grads(): lax.dot_general(window, flat_delta, (((0,), (0,)), ((), ())), preferred_e...  14.3 us
    dot_general x18, matrix products, convolve_back(): jnp.dot(window, weight[tap_row, tap_col].T, preferred_element_type=jnp.fl...  9.12 us
    dot_general x18, matrix products, convolve(): jnp.dot(window, weight[tap_row, tap_col], preferred_element_type=jnp.floa...  8.81 us
  transfers between devices with their start and end apart: 21, of which 5 were waited for; matrix products, arithmetic and copies ran while one was open for 4% of the time, Pallas kernels for 0%

commit v1 on v0

v1 whole, which is shorter than its diff:
```python
import functools
import math

import jax
import jax.numpy as jnp
from jax import lax
from jax.experimental import pallas as pl
from jax.experimental.pallas import tpu as pltpu
from jax.sharding import PartitionSpec as P

MESH = pl.DeviceIdType.MESH
BF = jnp.bfloat16
F32 = jnp.float32

ROWS = 32
COLS = 128
WIDE = 144
HID = 128
CROW = 4
CCOL = 8
CELLS = CROW * CCOL
PACK = 48
LO_J = 2
NUM_J = 9
PIECE = 5
TILES = 72
DIRS = [(dy, dx) for dy in (-1, 0, 1) for dx in (-1, 0, 1) if (dy, dx) != (0, 0)]


def dot(a, b):
    return jnp.dot(a, b, preferred_element_type=F32)


def dot_t(a, b):
    return lax.dot_general(a, b, (((0,), (0,)), ((), ())), preferred_element_type=F32)


def halves(x):
    hi = x.astype(BF)
    return hi, (x - hi.astype(F32)).astype(BF)


def spread_taps(w_ref, out_ref, back):
    zero = jnp.zeros((HID, HID), BF)
    for b in range(3):
        for a in range(3):
            block = w_ref[2 - a, 2 - b].T if back else w_ref[a, b]
            for s in range(2):
                k = a + s
                out_ref[pl.ds((k * 3 + b) * HID, HID), pl.ds(s * HID, HID)] = block
        out_ref[pl.ds(b * HID, HID), pl.ds(HID, HID)] = zero
        out_ref[pl.ds((9 + b) * HID, HID), pl.ds(0, HID)] = zero


def store_shifted(ref, pair, side, x):
    axis = x.ndim - 2
    ref[pair, side, :, pl.ds(HID, HID)] = x.astype(BF)
    ref[pair, side, :, pl.ds(0, HID)] = pltpu.roll(x, 1, axis).astype(BF)
    ref[pair, side, :, pl.ds(2 * HID, HID)] = pltpu.roll(x, WIDE - 1, axis).astype(BF)


def four_rows(ref, first, count, width):
    rows = [
        ref[pl.ds(first + k // 2, count), k % 2, pl.ds(0, width), :].reshape(count * width, 3 * HID)
        for k in range(4)
    ]
    return jnp.concatenate(rows, axis=-1)


def coarse_setup(lat, lon, nb_ref, cells_ref, rowmix_ref, colmix_ref):
    for block in range(9):
        dy, dx = block // 3, block % 3
        cells_ref[pl.ds(dy * CROW, CROW), pl.ds(dx * CCOL, CCOL), :] = (
            nb_ref[block, pl.ds(0, CELLS), :].astype(F32).reshape(CROW, CCOL, HID)
        )

    def line(block):
        return nb_ref[block, pl.ds(CELLS, 16), :].astype(F32)

    lane = lax.broadcasted_iota(jnp.int32, (16, HID), 1)
    rows = jnp.where(
        lane < 2,
        pltpu.roll(line(1), 98, 1),
        jnp.where(lane < 34, pltpu.roll(line(4), 2, 1), pltpu.roll(line(7), 34, 1)),
    )
    lane = lane[0:1]
    frac = rows[1:2] + rows[2:3] + rows[3:4]
    start = ((lane + 30) // 8 - 1).astype(F32)
    place = rows[0:1] - (lat * CROW - CROW).astype(F32) - start
    fine_row = lat * ROWS + lane - 2
    inside = ((fine_row >= 0) & (fine_row < 8 * ROWS)).astype(F32)
    for m in range(4):
        weight = jnp.where(place == float(m), 1.0 - frac, 0.0) + jnp.where(
            place == float(m - 1), frac, 0.0
        )
        rowmix_ref[pl.ds(m, 1), :] = weight * inside

    lane = lax.broadcasted_iota(jnp.int32, (16, HID), 1)
    edge = jnp.where(lane < 8, line(5), pltpu.roll(line(3), 16, 1))
    tables = []
    for part in (line(4), edge):
        frac = part[5:6] + part[6:7] + part[7:8]
        spot = part[4:5] - (lon * CCOL - CCOL).astype(F32)
        spot = jnp.where(spot < 0.0, spot + 128.0, spot)
        spot = jnp.where(spot >= 128.0, spot - 128.0, spot)
        cell = lax.broadcasted_iota(jnp.int32, (32, HID), 0).astype(F32)
        tables.append(
            jnp.where(cell == spot, 1.0 - frac, 0.0) + jnp.where(cell == spot + 1.0, frac, 0.0)
        )
    hi, lo = halves(jnp.concatenate(tables, axis=-1))
    colmix_ref[pl.ds(0, 32), :] = hi
    colmix_ref[pl.ds(32, 32), :] = lo


def lift(embed_ref, cells_ref, rowmix_ref, colmix_ref, mid_ref, l3_ref):
    window = cells_ref[...].reshape(12 * 24, HID).astype(BF)
    lifted = dot(window, embed_ref[...]).reshape(12, 24, HID)
    wide = jnp.concatenate([lifted[LO_J + j] for j in range(NUM_J)], axis=-1)
    wide = jnp.concatenate([wide, jnp.zeros((8, NUM_J * HID), F32)], axis=0)
    hi, lo = halves(wide)
    mixer = jnp.concatenate([colmix_ref[...], colmix_ref[pl.ds(0, 32), :]], axis=0)
    mid = dot_t(mixer, jnp.concatenate([hi, hi, lo], axis=0))
    mid_ref[...] = mid[0:WIDE]
    mix = rowmix_ref[...]
    for i in range(ROWS + 4):
        first = (i + 30) // 8 - 1 - LO_J
        total = None
        for m in range(4):
            weight = mix[m : m + 1, i : i + 1]
            term = weight * mid_ref[:, pl.ds((first + m) * HID, HID)]
            total = term if total is None else total + term
        store_shifted(l3_ref, i // 2, i % 2, total)


def spread_cot(lat, cot_ref, rowhalo_ref, colhalo_ref, c3_ref):
    near = lax.broadcasted_iota(jnp.int32, (16, HID), 0) < 8

    def put(i, own, scale):
        right = colhalo_ref[1, i].astype(F32)
        left = colhalo_ref[0, i].astype(F32)
        x = jnp.concatenate([own.astype(F32), jnp.where(near, right, left)], axis=0)
        if scale is not None:
            x = x * scale
        return x

    top = (lat > 0).astype(F32)
    bottom = (lat < 7).astype(F32)
    for t in range(2):
        store_shifted(c3_ref, 0, t, put(t, rowhalo_ref[0, t], top))
        store_shifted(c3_ref, 17, t, put(34 + t, rowhalo_ref[1, t], bottom))

    def step(q, carry):
        for t in range(2):
            r = 2 * q + t
            store_shifted(c3_ref, q + 1, t, put(r + 2, cot_ref[r], None))
        return carry

    lax.fori_loop(0, ROWS // 2, step, 0)


def middle(lat, first, count, l3_ref, c3_ref, w1_ref, w2t_ref, h3_ref, d3_ref):
    pre_all = dot(four_rows(l3_ref, first, count, WIDE), w1_ref[...])
    back_all = dot(four_rows(c3_ref, first, count, WIDE), w2t_ref[...])
    top = (lat > 0).astype(F32)
    bottom = (lat < 7).astype(F32)
    for p in range(count):
        for s in range(2):
            pre = pre_all[p * WIDE : (p + 1) * WIDE, s * HID : (s + 1) * HID]
            back = back_all[p * WIDE : (p + 1) * WIDE, s * HID : (s + 1) * HID]
            sig = 0.5 + 0.5 * jnp.tanh(0.5 * pre)
            hidden = pre * sig
            delta = back * (sig + hidden * (1.0 - sig))
            if first + p == 0 and s == 0:
                hidden, delta = hidden * top, delta * top
            if first + p == 16 and s == 1:
                hidden, delta = hidden * bottom, delta * bottom
            store_shifted(h3_ref, first + p, s, hidden)
            store_shifted(d3_ref, first + p, s, delta)


def rows_from(ref, start, lanes):
    q, odd = start // 2, start % 2
    if odd == 0:
        return ref[pl.ds(q, 16), :, pl.ds(0, COLS), lanes].reshape(ROWS * COLS, -1)
    parts = [ref[pl.ds(q, 16), 1, pl.ds(0, COLS), lanes], ref[pl.ds(q + 1, 16), 0, pl.ds(0, COLS), lanes]]
    return jnp.stack(parts, axis=1).reshape(ROWS * COLS, -1)


def weight_grad(v_ref, v_start, u_ref, u_start, out_ref):
    centre = pl.ds(HID, HID)
    left = jnp.concatenate([rows_from(v_ref, v_start + a, centre) for a in range(3)], axis=-1)
    right = rows_from(u_ref, u_start, pl.ds(0, 3 * HID))
    grad = dot_t(left, right)
    for a in range(3):
        for b in range(3):
            block = grad[a * HID : (a + 1) * HID, (2 - b) * HID : (3 - b) * HID]
            out_ref[pl.ds((a * 3 + b) * 8, 8)] = block.reshape(8, 16, HID).astype(BF)


def back_to_embed(first, count, d3_ref, w1t_ref, cot_ref, rowmix_ref, colmix_ref, down_ref):
    y = dot(four_rows(d3_ref, first, count, COLS), w1t_ref[...])
    rows = []
    for p in range(count):
        for s in range(2):
            part = y[p * COLS : (p + 1) * COLS, s * HID : (s + 1) * HID]
            rows.append((cot_ref[2 * (first + p) + s].astype(F32) + part).astype(BF))
    low = dot(colmix_ref[:, pl.ds(0, COLS)], jnp.concatenate(rows, axis=-1))
    low = low[0:32] + low[32:64]
    mix = rowmix_ref[...]
    sums = {}
    for n in range(2 * count):
        i = 2 * first + n + 2
        base = (i + 30) // 8 - 1
        part = low[:, n * HID : (n + 1) * HID]
        for m in range(4):
            term = mix[m : m + 1, i : i + 1] * part
            sums[base + m] = term if base + m not in sums else sums[base + m] + term
    for j, value in sums.items():
        down_ref[j] = down_ref[j] + value


def embed_grad(cells_ref, down_ref, out_ref):
    window = cells_ref[...].reshape(12 * 24, HID).astype(BF)
    down = jnp.concatenate([down_ref[j, pl.ds(0, 24), :] for j in range(12)], axis=0)
    hi, lo = halves(down)
    grad = dot_t(window, hi) + dot_t(window, lo)
    out_ref[...] = grad[0:80].reshape(PIECE, 16, HID).astype(BF)


def features_of(first, count, h3_ref, l3_ref, w2_ref, feat_ref):
    y = dot(four_rows(h3_ref, first, count, COLS), w2_ref[...])
    for p in range(count):
        for s in range(2):
            part = y[p * COLS : (p + 1) * COLS, s * HID : (s + 1) * HID]
            own = l3_ref[first + p + 1, s, pl.ds(0, COLS), pl.ds(HID, HID)].astype(F32)
            feat_ref[2 * (first + p) + s] = (own + part).astype(BF)


def ring(lat, lon, axis, step):
    if axis == "lat":
        return lax.rem(lat + step, 8), lon
    return lat, lax.rem(lon + step, 16)


class Exchange:
    def __init__(self, copies):
        self.copies = copies

    def start(self):
        for c in self.copies:
            c.start()

    def arrive(self):
        for c in self.copies:
            c.wait_recv()

    def sent(self):
        for c in self.copies:
            c.wait_send()


def remote(src, dst, send, recv, target):
    return pltpu.make_async_remote_copy(
        src_ref=src, dst_ref=dst, send_sem=send, recv_sem=recv, device_id=target, device_id_type=MESH
    )


class GradSum:
    def __init__(self, lat, lon, part, got, mine, other, final, sems):
        self.lat, self.lon = lat, lon
        self.part, self.got, self.mine, self.other, self.final = part, got, mine, other, final
        s_send, s_recv, l_send, l_recv, g_send, g_recv = sems
        spots = [ring(lat, lon, "lon", d) for d in range(1, 16)]
        own = pl.ds(lon * PIECE, PIECE)
        self.scatter = Exchange(
            [
                remote(part.at[pl.ds(t[1] * PIECE, PIECE)], got.at[n], s_send.at[n], s_recv.at[n], t)
                for n, t in enumerate(spots)
            ]
        )
        self.lats = Exchange(
            [
                remote(mine, other.at[d - 1], l_send.at[d - 1], l_recv.at[d - 1], ring(lat, lon, "lat", d))
                for d in range(1, 8)
            ]
        )
        self.gather = Exchange(
            [remote(final.at[own], final.at[own], g_send.at[n], g_recv.at[n], t) for n, t in enumerate(spots)]
        )

    def begin(self):
        self.scatter.start()

    def second(self):
        self.scatter.arrive()
        total = self.part[pl.ds(self.lon * PIECE, PIECE)].astype(F32)
        for n in range(15):
            total = total + self.got[n].astype(F32)
        self.mine[...] = total.astype(BF)
        self.lats.start()

    def third(self):
        self.lats.arrive()
        total = self.mine[...].astype(F32)
        for n in range(7):
            total = total + self.other[n].astype(F32)
        self.final[pl.ds(self.lon * PIECE, PIECE)] = total.astype(BF)
        self.gather.start()

    def finish(self, out_ref, scale):
        self.gather.arrive()
        for t in range(9):
            block = self.final[pl.ds(t * 8, 8)].astype(F32) * scale
            out_ref[t // 3, t % 3] = block.reshape(HID, HID)
        for e in (self.scatter, self.lats, self.gather):
            e.sent()


class SmallSum:
    def __init__(self, lat, lon, parts, slots, sems):
        self.parts, self.slots = parts, slots
        mate = lon + 1 - 2 * lax.rem(lon, 2)
        groups = [
            [ring(lat, lon, "lat", d) for d in range(1, 8)],
            [(lat, mate)],
            [ring(lat, lon, "lon", 2 * d) for d in range(1, 8)],
        ]
        self.steps = []
        base = 0
        for g, targets in enumerate(groups):
            copies = []
            for n, t in enumerate(targets):
                copies.append(remote(parts.at[g], slots.at[base + n], sems[0].at[base + n], sems[1].at[base + n], t))
            self.steps.append((base, len(targets), Exchange(copies)))
            base += len(targets)

    def begin(self, g):
        self.steps[g][2].start()

    def total(self, g):
        base, count, exchange = self.steps[g]
        exchange.arrive()
        total = self.parts[g].astype(F32)
        for n in range(count):
            total = total + self.slots[base + n].astype(F32)
        return total

    def pass_on(self, g):
        self.parts[g + 1] = self.total(g).astype(BF)
        self.begin(g + 1)

    def finish(self, out_ref, scale):
        out_ref[...] = (self.total(2) * scale).reshape(PIECE * 16, HID)
        for _, _, exchange in self.steps:
            exchange.sent()


def kernel(
    pack_ref, embed_ref, conv1_ref, conv2_ref, cot_ref,
    feat_ref, gemb_ref, g1_ref, g2_ref,
    nb_ref, rowhalo_ref, colhalo_ref, cells_ref, rowmix_ref, colmix_ref, mid_ref, down_ref,
    w1_ref, w2_ref, w1t_ref, w2t_ref, l3_ref, c3_ref, h3_ref, d3_ref,
    part1, got1, mine1, other1, final1, part2, got2, mine2, other2, final2, eparts, eslots,
    halo_send, halo_recv, cot_send, cot_recv, *sems,
):
    lat = lax.axis_index("lat")
    lon = lax.axis_index("lon")
    scale = 1.0 / math.sqrt(8 * ROWS * 16 * COLS)

    partners = [ring(lat, lon, "lat", d) for d in range(1, 8)]
    partners += [ring(lat, lon, "lon", d) for d in range(1, 16)]
    diagonal = {}
    for dy, dx in DIRS:
        spot = (lax.rem(lat + dy + 8, 8), lax.rem(lon + dx + 16, 16))
        diagonal[dy, dx] = spot
        if dy != 0 and dx != 0:
            partners.append(spot)
    barrier = pltpu.get_barrier_semaphore()
    for spot in partners:
        pl.semaphore_signal(barrier, inc=1, device_id=spot, device_id_type=MESH)
    pl.semaphore_wait(barrier, len(partners))

    packs, edges = [], []
    for n, (dy, dx) in enumerate(DIRS):
        slot = (1 - dy) * 3 + 1 - dx
        packs.append(remote(pack_ref, nb_ref.at[slot], halo_send.at[n], halo_recv.at[n], diagonal[dy, dx]))
        rows = {-1: pl.ds(0, 2), 0: pl.ds(0, ROWS), 1: pl.ds(ROWS - 2, 2)}[dy]
        if dx == 0:
            src = cot_ref.at[rows]
            dst = rowhalo_ref.at[0 if dy == 1 else 1]
        else:
            src = cot_ref.at[rows, pl.ds(0 if dx == -1 else COLS - 16, 16)]
            land = {1: pl.ds(0, 2), 0: pl.ds(2, ROWS), -1: pl.ds(ROWS + 2, 2)}[dy]
            dst = colhalo_ref.at[1 if dx == -1 else 0, land]
        edges.append(remote(src, dst, cot_send.at[n], cot_recv.at[n], diagonal[dy, dx]))
    packs, edges = Exchange(packs), Exchange(edges)
    packs.start()
    edges.start()

    sum1 = GradSum(lat, lon, part1, got1, mine1, other1, final1, sems[0:6])
    sum2 = GradSum(lat, lon, part2, got2, mine2, other2, final2, sems[6:12])
    small = SmallSum(lat, lon, eparts, eslots, sems[12:14])

    nb_ref[4] = pack_ref[...]
    spread_taps(conv1_ref, w1_ref, False)
    spread_taps(conv2_ref, w2_ref, False)
    spread_taps(conv1_ref, w1t_ref, True)
    spread_taps(conv2_ref, w2t_ref, True)
    down_ref[...] = jnp.zeros_like(down_ref)
    part1[pl.ds(TILES, 8)] = jnp.zeros((8, 16, HID), BF)
    part2[pl.ds(TILES, 8)] = jnp.zeros((8, 16, HID), BF)

    packs.arrive()
    coarse_setup(lat, lon, nb_ref, cells_ref, rowmix_ref, colmix_ref)
    lift(embed_ref, cells_ref, rowmix_ref, colmix_ref, mid_ref, l3_ref)
    edges.arrive()
    spread_cot(lat, cot_ref, rowhalo_ref, colhalo_ref, c3_ref)
    middle(lat, 0, 9, l3_ref, c3_ref, w1_ref, w2t_ref, h3_ref, d3_ref)
    middle(lat, 9, 8, l3_ref, c3_ref, w1_ref, w2t_ref, h3_ref, d3_ref)

    weight_grad(h3_ref, 0, c3_ref, 2, part2)
    sum2.begin()
    weight_grad(l3_ref, 1, d3_ref, 1, part1)
    sum1.begin()
    back_to_embed(0, 16, d3_ref, w1t_ref, cot_ref, rowmix_ref, colmix_ref, down_ref)
    embed_grad(cells_ref, down_ref, eparts.at[0])
    small.begin(0)
    sum2.second()
    features_of(0, 8, h3_ref, l3_ref, w2_ref, feat_ref)
    small.pass_on(0)
    sum1.second()
    features_of(8, 8, h3_ref, l3_ref, w2_ref, feat_ref)
    sum2.third()
    small.pass_on(1)
    sum1.third()
    sum2.finish(g2_ref, scale)
    small.finish(gemb_ref, scale)
    sum1.finish(g1_ref, scale)
    packs.sent()
    edges.sent()


def pack_block(coarse, row_src, row_frac, col_src, col_frac):
    def three(x):
        hi = x.astype(BF).astype(F32)
        mid = (x - hi).astype(BF).astype(F32)
        return [hi, mid, x - hi - mid]

    lines = [row_src.astype(F32)] + three(row_frac)
    lines = [jnp.pad(v, (0, HID - ROWS)) for v in lines]
    lines += [col_src.astype(F32)] + three(col_frac)
    lines = jnp.stack(lines + [jnp.zeros((HID,), F32)] * 8).astype(BF)
    cells = jnp.transpose(coarse, (1, 2, 0)).reshape(CELLS, -1)
    cells = jnp.pad(cells, ((0, 0), (0, HID - cells.shape[1])))
    return jnp.concatenate([cells, lines], axis=0)


def scratch_list():
    dma = pltpu.SemaphoreType.DMA
    wide = [pltpu.VMEM((12 * HID, 2 * HID), BF)] * 4
    grad = [
        pltpu.VMEM((80, 16, HID), BF),
        pltpu.VMEM((15, PIECE, 16, HID), BF),
        pltpu.VMEM((PIECE, 16, HID), BF),
        pltpu.VMEM((7, PIECE, 16, HID), BF),
        pltpu.VMEM((80, 16, HID), BF),
    ]
    return (
        [
            pltpu.VMEM((9, PACK, HID), BF),
            pltpu.VMEM((2, 2, COLS, HID), BF),
            pltpu.VMEM((2, ROWS + 4, 16, HID), BF),
            pltpu.VMEM((12, 24, HID), F32),
            pltpu.VMEM((8, HID), F32),
            pltpu.VMEM((64, 2 * HID), BF),
            pltpu.VMEM((WIDE, NUM_J * HID), F32),
            pltpu.VMEM((12, 32, HID), F32),
        ]
        + wide
        + [
            pltpu.VMEM((18, 2, WIDE, 3 * HID), BF),
            pltpu.VMEM((18, 2, WIDE, 3 * HID), BF),
            pltpu.VMEM((17, 2, WIDE, 3 * HID), BF),
            pltpu.VMEM((17, 2, WIDE, 3 * HID), BF),
        ]
        + grad
        + grad
        + [pltpu.VMEM((3, PIECE, 16, HID), BF), pltpu.VMEM((15, PIECE, 16, HID), BF)]
        + [dma((8,))] * 4
        + [dma((15,)), dma((15,)), dma((7,)), dma((7,)), dma((15,)), dma((15,))] * 2
        + [dma((15,))] * 2
    )


def on_device(coarse, row_src, row_frac, col_src, col_frac, embed_weight, conv1_weight, conv2_weight, cotangent):
    pack = pack_block(coarse, row_src, row_frac, col_src, col_frac)
    embed = jnp.pad(embed_weight, ((0, HID - embed_weight.shape[0]), (0, 0)))
    vmem = pl.BlockSpec(memory_space=pltpu.VMEM)
    conv = jax.ShapeDtypeStruct((3, 3, HID, HID), F32)
    features, grad_embed, grad_conv1, grad_conv2 = pl.pallas_call(
        kernel,
        out_shape=[
            jax.ShapeDtypeStruct((ROWS, COLS, HID), BF),
            jax.ShapeDtypeStruct((PIECE * 16, HID), F32),
            conv,
            conv,
        ],
        in_specs=[vmem] * 5,
        out_specs=[vmem] * 4,
        scratch_shapes=scratch_list(),
        compiler_params=pltpu.CompilerParams(
            collective_id=0, has_side_effects=True, vmem_limit_bytes=56 * 2**20
        ),
    )(pack, embed, conv1_weight, conv2_weight, cotangent)
    return (features, grad_embed[: coarse.shape[0]], grad_conv1, grad_conv2)


def solution(mesh):
    in_specs = (
        P(None, "lat", "lon"),
        P("lat"),
        P("lat"),
        P("lon"),
        P("lon"),
        P(),
        P(),
        P(),
        P("lat", "lon", None),
    )
    out_specs = (P("lat", "lon", None), P(), P(), P())
    return jax.shard_map(
        on_device, mesh=mesh, in_specs=in_specs, out_specs=out_specs, check_vma=False
    )
```

time: 362 us -> 68.7 us (0.19); the launches traced: 358 us -> 68.4 us
  waiting for transfers between devices: 138 us -> 0 us
  blocking collectives: 69.8 us -> 0 us
  Pallas kernels: 0 us -> 57.5 us
  starting transfers between devices: 54.5 us -> 0 us
  matrix products: 37 us -> 0 us
  local copies, waits for them, and re-layouts: 29.7 us -> 10.2 us
  between operations: 14.9 us -> 0.7 us
  other arithmetic: 14.1 us -> 0.02 us
    psum x1 -> x0, waiting for transfers between devices: 134 us -> none  [on_device(): totals = lax.psum((terms[0], terms[1], terms[2]), ('lat', 'lon'))]
    psum x1 -> x0, blocking collectives: 69.8 us -> none  [on_device(): totals = lax.psum((terms[0], terms[1], terms[2]), ('lat', 'lon'))]
    pallas_call x0 -> x1, Pallas kernels: none -> 57.5 us  [on_device(): pl.pallas_call(kernel, out_shape=[jax.ShapeDtypeStruct((ROWS, COLS, HID),...]
    ppermute x20 -> x0, starting transfers between devices: 54.5 us -> none  [the longest x10 39.3 us: with_halo(): after = lax.ppermute(first, axis, down)]
    dot_general x58 -> x0, matrix products: 37 us -> none  [the longest x18 14.3 us: weight_grads(): lax.dot_general(window, flat_delta, (((0,), (0,)), ((), ())), preferred_e...]
    slice x10 -> x0, local copies, waits for them, and re-layouts: 13.4 us -> none  [the longest x2 7.97 us: convolve_back(): padded[2 - tap_row:2 - tap_row + span_rows, 2 - tap_col:2 - tap_col + spa...]
    unnamed x50 -> x22, local copies, waits for them, and re-layouts: 16 us -> 7.72 us
    mul x4 -> x0, other arithmetic: 6.17 us -> none  [the longest x2 4.43 us: edge_zero(): return padded * keep.astype(padded.dtype)[:, None, None]]
  transfers between devices with their start and end apart: 21 -> 0, of which waited for: 5 -> 0; matrix products, arithmetic and copies ran while one was open for 4% -> 0% of each run, Pallas kernels for 0% -> 0%
where the time goes in v1:
time: 68.7 us; the launch traced here: 68.4 us
  Pallas kernels  57.5 us (84%)
  local copies, waits for them, and re-layouts  10.2 us (15%)
  between operations  0.7 us (1%)
    pallas_call x1, Pallas kernels, on_device(): pl.pallas_call(kernel, out_shape=[jax.ShapeDtypeStruct((ROWS, COLS, HID),...  57.5 us
    unnamed x22, local copies, waits for them, and re-layouts  7.72 us
    concatenate x1, local copies, waits for them, and re-layouts, pack_block(): return jnp.concatenate([cells, lines], axis=0)  1.79 us

profile of v1, /device:TPU:1, one launch (start us, length us, event | category | flops | bytes accessed | tf_op | source)
XLA Modules:
  0.0 68.4 jit_solution(10045297159033912256)
XLA Ops:
  0.6 0.0 copy-start.7
  0.6 0.6 copy-done.7
  1.3 0.0 copy-start.8
  1.3 0.6 copy-done.8
  1.9 0.0 copy-start.5
  1.9 0.6 copy-done.5
  2.6 0.0 copy-start.6
  2.6 0.0 copy-start.4
  2.6 0.6 copy-done.6
  3.3 0.1 copy-done.4
  3.3 0.0 copy-start.3
  3.3 1.8 %concatenate.4.pack_ref = bf16[48,128]{1,0:T(8,128)(2,1)} concatenate(bf16[32,128]{1,0:T(8,128)(2,1)S(1)} %pad.25, bf16[1,128]{1,0:T(2,128)(2,1)S(1)} %get-tuple-element.21, bf16[1,128]{1,0:T(2,128)(2,1)S(1)} %get-tuple-element.20, bf16[1,128]{1,0:T(2,128)(2,1)S(1)} %get-tuple-element.19, bf16[1,128]{1,0:T(2,128)(2,1)S(1)} %get-tuple-element.18, ...), dimensions={0} | concatenate | bytes 24576 | tf_op jit(solution)/shard_map/concatenate | solution.py:455
  5.1 0.0 copy-done.3
  5.1 0.6 pad.30.embed_ref
  5.8 57.5 %shard_map.120 = (bf16[32,128,128]{2,1,0:T(8,128)(2,1)}, f32[80,128]{1,0:T(8,128)}, f32[3,3,128,128]{3,2,1,0:T(8,128)}, f32[3,3,128,128]{3,2,1,0:T(8,128)}) custom-call(bf16[48,128]{1,0:T(8,128)(2,1)} %concatenate.4.pack_ref, bf16[128,128]{1,0:T(8,128)(2,1)} %pad.30.embed_ref, bf16[3,3,128,128]{3,2,1,0:T(8,128)(2,1)} %conv1_ref.1, ...), custom_call_target="tpu_custom_call" | custom-call | tf_op jit(solution)/shard_map/pallas_call | solution.py:500
  63.3 0.0 copy-start.2
  63.3 0.0 copy-start.1
  63.3 2.4 %copy.17 = bf16[32,128,128]{2,1,0:T(8,128)(2,1)} copy(bf16[32,128,128]{2,1,0:T(8,128)(2,1)} %get-tuple-element.26) | data formatting | bytes 2097152
  65.7 0.0 copy-done.2
  65.7 0.6 copy.18
  66.3 0.0 copy-done.1
  66.3 0.0 copy-start
  66.3 0.8 %copy.19 = f32[3,3,128,128]{3,2,1,0:T(8,128)} copy(f32[3,3,128,128]{3,2,1,0:T(8,128)S(1)} %copy-done.1) | data formatting | bytes 1179648
  67.1 0.5 copy-done
  67.6 0.8 %copy.20 = f32[3,3,128,128]{3,2,1,0:T(8,128)} copy(f32[3,3,128,128]{3,2,1,0:T(8,128)S(1)} %copy-done) | data formatting | bytes 1179648
  (8 shorter events, 0.0 us)
Async XLA Ops:
  0.6 0.7 copy-start.7
  1.3 0.7 copy-start.8
  1.9 0.7 copy-start.5
  2.6 0.7 copy-start.6
  2.6 0.7 %copy-start.4 = (bf16[73,4,8]{0,2,1:T(8,128)(2,1)S(1)}, bf16[73,4,8]{0,2,1:T(8,128)(2,1)}, u32[]{:S(2)}) copy-start(bf16[73,4,8]{0,2,1:T(8,128)(2,1)} %param.9) | copy-start | bytes 14020
  3.3 1.8 %copy-start.3 = (bf16[73,128]{1,0:T(8,128)(2,1)S(1)}, bf16[73,128]{1,0:T(8,128)(2,1)}, u32[]{:S(2)}) copy-start(bf16[73,128]{1,0:T(8,128)(2,1)} %param.14) | copy-start | bytes 56068
  63.3 2.4 %copy-start.2 = (f32[80,128]{1,0:T(8,128)S(1)}, f32[80,128]{1,0:T(8,128)}, u32[]{:S(2)}) copy-start(f32[80,128]{1,0:T(8,128)} %get-tuple-element.9) | copy-start | bytes 122884
  63.3 3.0 %copy-start.1 = (f32[3,3,128,128]{3,2,1,0:T(8,128)S(1)}, f32[3,3,128,128]{3,2,1,0:T(8,128)}, u32[]{:S(2)}) copy-start(f32[3,3,128,128]{3,2,1,0:T(8,128)} %get-tuple-element.28) | copy-start | bytes 1769476
  66.3 1.3 %copy-start = (f32[3,3,128,128]{3,2,1,0:T(8,128)S(1)}, f32[3,3,128,128]{3,2,1,0:T(8,128)}, u32[]{:S(2)}) copy-start(f32[3,3,128,128]{3,2,1,0:T(8,128)} %get-tuple-element.29) | copy-start | bytes 1769476

commit v2 on v1

v2 whole, which is shorter than its diff:
```python
import functools
import math

import jax
import jax.numpy as jnp
from jax import lax
from jax.experimental import pallas as pl
from jax.experimental.pallas import tpu as pltpu
from jax.sharding import PartitionSpec as P

MESH = pl.DeviceIdType.MESH
BF = jnp.bfloat16
F32 = jnp.float32

ROWS = 32
COLS = 128
WIDE = 144
HID = 128
CROW = 4
CCOL = 8
CELLS = CROW * CCOL
PACK = 48
LO_J = 2
NUM_J = 9
TILES = 72
HALF = 36
PIECE = 3
EMBED_TILES = 5
DIRS = [(dy, dx) for dy in (-1, 0, 1) for dx in (-1, 0, 1) if (dy, dx) != (0, 0)]


def dot(a, b):
    return jnp.dot(a, b, preferred_element_type=F32)


def dot_t(a, b):
    return lax.dot_general(a, b, (((0,), (0,)), ((), ())), preferred_element_type=F32)


def halves(x):
    hi = x.astype(BF)
    return hi, (x - hi.astype(F32)).astype(BF)


def spread_taps(w_ref, out_ref, back):
    zero = jnp.zeros((HID, HID), BF)
    for b in range(3):
        for a in range(3):
            block = w_ref[2 - a, 2 - b].T if back else w_ref[a, b]
            for s in range(2):
                k = a + s
                out_ref[pl.ds((k * 3 + b) * HID, HID), pl.ds(s * HID, HID)] = block
        out_ref[pl.ds(b * HID, HID), pl.ds(HID, HID)] = zero
        out_ref[pl.ds((9 + b) * HID, HID), pl.ds(0, HID)] = zero


def store_shifted(ref, pair, side, x):
    axis = x.ndim - 2
    ref[pair, side, :, pl.ds(HID, HID)] = x.astype(BF)
    ref[pair, side, :, pl.ds(0, HID)] = pltpu.roll(x, 1, axis).astype(BF)
    ref[pair, side, :, pl.ds(2 * HID, HID)] = pltpu.roll(x, WIDE - 1, axis).astype(BF)


def four_rows(ref, first, count, width, start=0):
    rows = [
        ref[pl.ds(first + k // 2, count), k % 2, pl.ds(start, width), :].reshape(count * width, 3 * HID)
        for k in range(4)
    ]
    return jnp.concatenate(rows, axis=-1)


def coarse_setup(lat, lon, nb_ref, cells_ref, rowmix_ref, colmix_ref):
    for block in range(9):
        dy, dx = block // 3, block % 3
        cells_ref[pl.ds(dy * CROW, CROW), pl.ds(dx * CCOL, CCOL), :] = (
            nb_ref[block, pl.ds(0, CELLS), :].astype(F32).reshape(CROW, CCOL, HID)
        )

    def line(block):
        return nb_ref[block, pl.ds(CELLS, 16), :].astype(F32)

    lane = lax.broadcasted_iota(jnp.int32, (16, HID), 1)
    rows = jnp.where(
        lane < 2,
        pltpu.roll(line(1), 98, 1),
        jnp.where(lane < 34, pltpu.roll(line(4), 2, 1), pltpu.roll(line(7), 34, 1)),
    )
    lane = lane[0:1]
    frac = rows[1:2] + rows[2:3] + rows[3:4]
    start = ((lane + 30) // 8 - 1).astype(F32)
    place = rows[0:1] - (lat * CROW - CROW).astype(F32) - start
    fine_row = lat * ROWS + lane - 2
    inside = ((fine_row >= 0) & (fine_row < 8 * ROWS)).astype(F32)
    for m in range(4):
        weight = jnp.where(place == float(m), 1.0 - frac, 0.0) + jnp.where(
            place == float(m - 1), frac, 0.0
        )
        rowmix_ref[pl.ds(m, 1), :] = weight * inside

    lane = lax.broadcasted_iota(jnp.int32, (16, HID), 1)
    edge = jnp.where(lane < 8, line(5), pltpu.roll(line(3), 16, 1))
    tables = []
    for part in (line(4), edge):
        frac = part[5:6] + part[6:7] + part[7:8]
        spot = part[4:5] - (lon * CCOL - CCOL).astype(F32)
        spot = jnp.where(spot < 0.0, spot + 128.0, spot)
        spot = jnp.where(spot >= 128.0, spot - 128.0, spot)
        cell = lax.broadcasted_iota(jnp.int32, (32, HID), 0).astype(F32)
        tables.append(
            jnp.where(cell == spot, 1.0 - frac, 0.0) + jnp.where(cell == spot + 1.0, frac, 0.0)
        )
    hi, lo = halves(jnp.concatenate(tables, axis=-1))
    colmix_ref[pl.ds(0, 32), :] = hi
    colmix_ref[pl.ds(32, 32), :] = lo


def lift(embed_ref, cells_ref, rowmix_ref, colmix_ref, mid_ref, l3_ref):
    cells = [cells_ref[LO_J + j] for j in range(NUM_J)]
    wide = jnp.concatenate(cells, axis=-1)
    wide = jnp.concatenate([wide, jnp.zeros((8, NUM_J * HID), F32)], axis=0).astype(BF)
    mid = dot_t(colmix_ref[...], jnp.concatenate([wide, wide], axis=0))
    mid_ref[...] = mid[0:WIDE]
    mix = rowmix_ref[...]
    for start in range(0, ROWS + 4, 12):
        rows = []
        for i in range(start, start + 12):
            first = (i + 30) // 8 - 1 - LO_J
            total = None
            for m in range(4):
                weight = mix[m : m + 1, i : i + 1]
                term = weight * mid_ref[:, pl.ds((first + m) * HID, HID)]
                total = term if total is None else total + term
            rows.append(total.astype(BF))
        lifted = dot(jnp.concatenate(rows, axis=0), embed_ref[...])
        for n in range(12):
            i = start + n
            store_shifted(l3_ref, i // 2, i % 2, lifted[n * WIDE : (n + 1) * WIDE])


def spread_own(cot_ref, c3_ref):
    def step(q, carry):
        for t in range(2):
            x = cot_ref[2 * q + t].astype(F32)
            own = pl.ds(0, COLS)
            c3_ref[q + 1, t, own, pl.ds(HID, HID)] = cot_ref[2 * q + t]
            c3_ref[q + 1, t, own, pl.ds(0, HID)] = pltpu.roll(x, 1, 0).astype(BF)
            c3_ref[q + 1, t, own, pl.ds(2 * HID, HID)] = pltpu.roll(x, COLS - 1, 0).astype(BF)
        return carry

    lax.fori_loop(0, ROWS // 2, step, 0)


def close_edges(lat, cot_ref, rowhalo_ref, colhalo_ref, c3_ref):
    near = lax.broadcasted_iota(jnp.int32, (16, HID), 0) < 8

    def beside(i):
        return jnp.where(near, colhalo_ref[1, i].astype(F32), colhalo_ref[0, i].astype(F32))

    top = (lat > 0).astype(F32)
    bottom = (lat < 7).astype(F32)
    for t in range(2):
        x = jnp.concatenate([rowhalo_ref[0, t].astype(F32), beside(t)], axis=0)
        store_shifted(c3_ref, 0, t, x * top)
        x = jnp.concatenate([rowhalo_ref[1, t].astype(F32), beside(ROWS + 2 + t)], axis=0)
        store_shifted(c3_ref, 17, t, x * bottom)

    def step(q, carry):
        for t in range(2):
            r = 2 * q + t
            last = cot_ref[r, pl.ds(COLS - 16, 16)].astype(F32)
            first = cot_ref[r, pl.ds(0, 16)].astype(F32)
            x = jnp.concatenate([last, beside(r + 2), first], axis=0)
            west = pltpu.roll(x, 1, 0).astype(BF)
            east = pltpu.roll(x, 47, 0).astype(BF)
            wide = pl.ds(COLS, 16)
            c3_ref[q + 1, t, wide, pl.ds(HID, HID)] = x[16:32].astype(BF)
            c3_ref[q + 1, t, wide, pl.ds(0, HID)] = west[16:32]
            c3_ref[q + 1, t, pl.ds(0, 16), pl.ds(0, HID)] = west[32:48]
            c3_ref[q + 1, t, pl.ds(COLS - 16, 32), pl.ds(2 * HID, HID)] = east[0:32]
        return carry

    lax.fori_loop(0, ROWS // 2, step, 0)


def back_inside(c3_ref, w2t_ref, back_ref):
    y = dot(four_rows(c3_ref, 1, 15, 96, 16), w2t_ref[...])
    back_ref[pl.ds(1, 15), pl.ds(16, 96), :] = y.reshape(15, 96, 2 * HID)


def back_around(c3_ref, w2t_ref, back_ref):
    parts = [
        four_rows(c3_ref, 1, 15, 16, 0),
        four_rows(c3_ref, 1, 15, 32, COLS - 16),
        four_rows(c3_ref, 0, 1, WIDE),
        four_rows(c3_ref, 16, 1, WIDE),
    ]
    y = dot(jnp.concatenate(parts, axis=0), w2t_ref[...])
    back_ref[pl.ds(1, 15), pl.ds(0, 16), :] = y[0:240].reshape(15, 16, 2 * HID)
    back_ref[pl.ds(1, 15), pl.ds(COLS - 16, 32), :] = y[240:720].reshape(15, 32, 2 * HID)
    back_ref[0] = y[720 : 720 + WIDE]
    back_ref[16] = y[720 + WIDE : 720 + 2 * WIDE]


def middle(lat, first, count, l3_ref, back_ref, w1_ref, h3_ref, d3_ref):
    pre_all = dot(four_rows(l3_ref, first, count, WIDE), w1_ref[...])
    top = (lat > 0).astype(F32)
    bottom = (lat < 7).astype(F32)
    for p in range(count):
        for s in range(2):
            pre = pre_all[p * WIDE : (p + 1) * WIDE, s * HID : (s + 1) * HID]
            back = back_ref[first + p, :, pl.ds(s * HID, HID)]
            sig = 0.5 + 0.5 * jnp.tanh(0.5 * pre)
            hidden = pre * sig
            delta = back * (sig + hidden * (1.0 - sig))
            if first + p == 0 and s == 0:
                hidden, delta = hidden * top, delta * top
            if first + p == 16 and s == 1:
                hidden, delta = hidden * bottom, delta * bottom
            store_shifted(h3_ref, first + p, s, hidden)
            store_shifted(d3_ref, first + p, s, delta)


def rows_from(ref, start, lanes):
    q, odd = start // 2, start % 2
    if odd == 0:
        return ref[pl.ds(q, 16), :, pl.ds(0, COLS), lanes].reshape(ROWS * COLS, -1)
    parts = [ref[pl.ds(q, 16), 1, pl.ds(0, COLS), lanes], ref[pl.ds(q + 1, 16), 0, pl.ds(0, COLS), lanes]]
    return jnp.stack(parts, axis=1).reshape(ROWS * COLS, -1)


def weight_grad(v_ref, v_start, u_ref, u_start, out_ref):
    centre = pl.ds(HID, HID)
    left = jnp.concatenate([rows_from(v_ref, v_start + a, centre) for a in range(3)], axis=-1)
    right = rows_from(u_ref, u_start, pl.ds(0, 3 * HID))
    grad = dot_t(left, right)
    for a in range(3):
        for b in range(3):
            block = grad[a * HID : (a + 1) * HID, (2 - b) * HID : (3 - b) * HID]
            out_ref[pl.ds((a * 3 + b) * 8, 8)] = block.reshape(8, 16, HID).astype(BF)


def back_to_embed(first, count, d3_ref, w1t_ref, cot_ref, rowmix_ref, colmix_ref, down_ref):
    y = dot(four_rows(d3_ref, first, count, COLS), w1t_ref[...])
    rows = []
    for p in range(count):
        for s in range(2):
            part = y[p * COLS : (p + 1) * COLS, s * HID : (s + 1) * HID]
            rows.append((cot_ref[2 * (first + p) + s].astype(F32) + part).astype(BF))
    low = dot(colmix_ref[:, pl.ds(0, COLS)], jnp.concatenate(rows, axis=-1))
    low = low[0:32] + low[32:64]
    mix = rowmix_ref[...]
    sums = {}
    for n in range(2 * count):
        i = 2 * first + n + 2
        base = (i + 30) // 8 - 1
        part = low[:, n * HID : (n + 1) * HID]
        for m in range(4):
            term = mix[m : m + 1, i : i + 1] * part
            sums[base + m] = term if base + m not in sums else sums[base + m] + term
    for j, value in sums.items():
        down_ref[j] = down_ref[j] + value


def embed_grad(cells_ref, down_ref, out_ref):
    window = cells_ref[...].reshape(12 * 24, HID).astype(BF)
    down = jnp.concatenate([down_ref[j, pl.ds(0, 24), :] for j in range(12)], axis=0)
    hi, lo = halves(down)
    grad = dot_t(window, hi) + dot_t(window, lo)
    out_ref[...] = grad[0 : EMBED_TILES * 16].reshape(EMBED_TILES, 16, HID).astype(BF)


def features_of(first, count, h3_ref, l3_ref, w2_ref, feat_ref):
    y = dot(four_rows(h3_ref, first, count, COLS), w2_ref[...])
    for p in range(count):
        for s in range(2):
            part = y[p * COLS : (p + 1) * COLS, s * HID : (s + 1) * HID]
            own = l3_ref[first + p + 1, s, pl.ds(0, COLS), pl.ds(HID, HID)].astype(F32)
            feat_ref[2 * (first + p) + s] = (own + part).astype(BF)


class Place:
    def __init__(self):
        self.lat = lax.axis_index("lat")
        self.lon = lax.axis_index("lon")
        self.core = lax.rem(self.lon, 2)
        self.z = lax.rem(self.lat, 2) * 2 + lax.rem(self.lon // 2, 2)
        self.plane = self.lon // 4 * 4 + self.lat // 2
        self.mate = (self.lat, self.lon + 1 - 2 * self.core)
        self.planes = [lax.rem(self.plane + d, 16) for d in range(1, 16)]
        self.plane_mates = [self.spot(q, self.z) for q in self.planes]
        self.z_mates = [self.spot(self.plane, lax.rem(self.z + d, 4)) for d in range(1, 4)]
        self.around = [(lax.rem(self.lat + dy + 8, 8), lax.rem(self.lon + dx + 16, 16)) for dy, dx in DIRS]

    def spot(self, plane, z):
        return (lax.rem(plane, 4) * 2 + z // 2, plane // 4 * 4 + lax.rem(z, 2) * 2 + self.core)


class Exchange:
    def __init__(self, copies):
        self.copies = copies

    def start(self):
        for c in self.copies:
            c.start()

    def arrive(self):
        for c in self.copies:
            c.wait_recv()

    def sent(self):
        for c in self.copies:
            c.wait_send()


def remote(src, dst, send, recv, target):
    return pltpu.make_async_remote_copy(
        src_ref=src, dst_ref=dst, send_sem=send, recv_sem=recv, device_id=target, device_id_type=MESH
    )


class GradSum:
    def __init__(self, place, part, paired, half, got, mine, other, final, twin, sems):
        self.part, self.paired, self.half, self.got = part, paired, half, got
        self.mine, self.other, self.final, self.twin = mine, other, final, twin
        a_sem, s_send, s_recv, z_send, z_recv, g_send, g_recv = sems
        self.keep = place.core * HALF
        self.own = pl.ds(place.plane * PIECE, PIECE)
        away = part.at[pl.ds(HALF - self.keep, HALF)]
        self.pair = Exchange([remote(away, paired, a_sem.at[0], a_sem.at[1], place.mate)])
        self.scatter = Exchange(
            [
                remote(half.at[pl.ds(q * PIECE, PIECE)], got.at[n], s_send.at[n], s_recv.at[n], t)
                for n, (q, t) in enumerate(zip(place.planes, place.plane_mates))
            ]
        )
        self.column = Exchange(
            [remote(mine, other.at[n], z_send.at[n], z_recv.at[n], t) for n, t in enumerate(place.z_mates)]
        )
        self.gather = Exchange(
            [
                remote(final.at[self.own], final.at[self.own], g_send.at[n], g_recv.at[n], t)
                for n, t in enumerate(place.plane_mates)
            ]
        )
        self.swap = Exchange([remote(final.at[pl.ds(0, HALF)], twin, a_sem.at[2], a_sem.at[3], place.mate)])

    def step_pair(self):
        self.pair.start()

    def step_scatter(self):
        self.pair.arrive()
        total = self.part[pl.ds(self.keep, HALF)].astype(F32) + self.paired[...].astype(F32)
        self.half[pl.ds(0, HALF)] = total.astype(BF)
        self.half[pl.ds(HALF, 16 * PIECE - HALF)] = jnp.zeros((16 * PIECE - HALF, 16, HID), BF)
        self.scatter.start()

    def step_column(self):
        self.scatter.arrive()
        total = self.half[self.own].astype(F32)
        for n in range(15):
            total = total + self.got[n].astype(F32)
        self.mine[...] = total.astype(BF)
        self.column.start()

    def step_gather(self):
        self.column.arrive()
        total = self.mine[...].astype(F32)
        for n in range(3):
            total = total + self.other[n].astype(F32)
        self.final[self.own] = total.astype(BF)
        self.gather.start()

    def step_swap(self, out_ref, scale):
        self.gather.arrive()
        self.swap.start()
        out_ref[pl.ds(self.keep, HALF)] = self.final[pl.ds(0, HALF)].astype(F32) * scale

    def finish(self, out_ref, scale):
        self.swap.arrive()
        out_ref[pl.ds(HALF - self.keep, HALF)] = self.twin[...].astype(F32) * scale
        for e in (self.pair, self.scatter, self.column, self.gather, self.swap):
            e.sent()


class SmallSum:
    def __init__(self, place, parts, slots, sems):
        self.parts, self.slots = parts, slots
        self.steps = []
        base = 0
        for g, targets in enumerate([[place.mate], place.z_mates, place.plane_mates]):
            copies = []
            for n, t in enumerate(targets):
                copies.append(remote(parts.at[g], slots.at[base + n], sems[0].at[base + n], sems[1].at[base + n], t))
            self.steps.append((base, len(targets), Exchange(copies)))
            base += len(targets)

    def begin(self, g):
        self.steps[g][2].start()

    def total(self, g):
        base, count, exchange = self.steps[g]
        exchange.arrive()
        total = self.parts[g].astype(F32)
        for n in range(count):
            total = total + self.slots[base + n].astype(F32)
        return total

    def pass_on(self, g):
        self.parts[g + 1] = self.total(g).astype(BF)
        self.begin(g + 1)

    def finish(self, out_ref, scale):
        out_ref[...] = (self.total(2) * scale).reshape(EMBED_TILES * 16, HID)
        for _, _, exchange in self.steps:
            exchange.sent()


def pack_block(coarse_ref, row_src_ref, row_frac_ref, col_src_ref, col_frac_ref, lines_ref, pack_ref):
    pack_ref[...] = jnp.zeros_like(pack_ref)
    pack_ref[pl.ds(0, CELLS), pl.ds(0, coarse_ref.shape[1])] = coarse_ref[...]
    lines_ref[...] = jnp.zeros_like(lines_ref)
    for row, src_ref, frac_ref in ((0, row_src_ref, row_frac_ref), (4, col_src_ref, col_frac_ref)):
        lanes = pl.ds(0, src_ref.shape[1])
        lines_ref[pl.ds(row, 1), lanes] = src_ref[...].astype(F32)
        left = frac_ref[...]
        for n in range(1, 4):
            term = left.astype(BF).astype(F32)
            lines_ref[pl.ds(row + n, 1), lanes] = term
            left = left - term
    pack_ref[pl.ds(CELLS, 16), :] = lines_ref[...].astype(BF)


def kernel(
    coarse_hbm, row_src_hbm, row_frac_hbm, col_src_hbm, col_frac_hbm, embed_hbm, conv1_hbm, conv2_hbm, cot_hbm,
    feat_ref, gemb_ref, g1_ref, g2_ref,
    coarse_ref, row_src_ref, row_frac_ref, col_src_ref, col_frac_ref, embed_in_ref, conv1_ref, conv2_ref, cot_ref,
    lines_ref, pack_ref, embed_ref,
    nb_ref, rowhalo_ref, colhalo_ref, cells_ref, rowmix_ref, colmix_ref, mid_ref, down_ref,
    w1_ref, w2_ref, w1t_ref, w2t_ref, l3_ref, c3_ref, h3_ref, d3_ref, back_ref,
    part1, paired1, half1, got1, mine1, other1, final1, twin1,
    part2, paired2, half2, got2, mine2, other2, final2, twin2, eparts, eslots,
    load_sem, halo_send, halo_recv, cot_send, cot_recv, *sems,
):
    place = Place()
    lat, lon = place.lat, place.lon
    scale = 1.0 / math.sqrt(8 * ROWS * 16 * COLS)

    barrier = pltpu.get_barrier_semaphore()
    partners = [place.mate] + place.around + place.z_mates + place.plane_mates
    for spot in partners:
        pl.semaphore_signal(barrier, inc=1, device_id=spot, device_id_type=MESH)

    pairs = [
        (coarse_hbm, coarse_ref), (row_src_hbm, row_src_ref), (row_frac_hbm, row_frac_ref),
        (col_src_hbm, col_src_ref), (col_frac_hbm, col_frac_ref), (cot_hbm, cot_ref),
        (conv2_hbm, conv2_ref), (conv1_hbm, conv1_ref), (embed_hbm, embed_in_ref),
    ]
    loads = [pltpu.make_async_copy(src, dst, load_sem.at[n]) for n, (src, dst) in enumerate(pairs)]
    for load in loads:
        load.start()

    packs, edges = [], []
    for n, (dy, dx) in enumerate(DIRS):
        slot = (1 - dy) * 3 + 1 - dx
        packs.append(remote(pack_ref, nb_ref.at[slot], halo_send.at[n], halo_recv.at[n], place.around[n]))
        rows = {-1: pl.ds(0, 2), 0: pl.ds(0, ROWS), 1: pl.ds(ROWS - 2, 2)}[dy]
        if dx == 0:
            src = cot_ref.at[rows]
            dst = rowhalo_ref.at[0 if dy == 1 else 1]
        else:
            src = cot_ref.at[rows, pl.ds(0 if dx == -1 else COLS - 16, 16)]
            land = {1: pl.ds(0, 2), 0: pl.ds(2, ROWS), -1: pl.ds(ROWS + 2, 2)}[dy]
            dst = colhalo_ref.at[1 if dx == -1 else 0, land]
        edges.append(remote(src, dst, cot_send.at[n], cot_recv.at[n], place.around[n]))
    packs, edges = Exchange(packs), Exchange(edges)
    sum1 = GradSum(place, part1, paired1, half1, got1, mine1, other1, final1, twin1, sems[0:7])
    sum2 = GradSum(place, part2, paired2, half2, got2, mine2, other2, final2, twin2, sems[7:14])
    small = SmallSum(place, eparts, eslots, sems[14:16])

    for load in loads[0:5]:
        load.wait()
    pack_block(coarse_ref, row_src_ref, row_frac_ref, col_src_ref, col_frac_ref, lines_ref, pack_ref)
    loads[5].wait()
    pl.semaphore_wait(barrier, len(partners))
    packs.start()
    edges.start()

    nb_ref[4] = pack_ref[...]
    for load in loads[6:9]:
        load.wait()
    spread_taps(conv2_ref, w2t_ref, True)
    spread_own(cot_ref, c3_ref)
    back_inside(c3_ref, w2t_ref, back_ref)
    spread_taps(conv1_ref, w1_ref, False)
    spread_taps(conv2_ref, w2_ref, False)
    spread_taps(conv1_ref, w1t_ref, True)
    embed_ref[...] = jnp.zeros_like(embed_ref)
    embed_ref[pl.ds(0, embed_in_ref.shape[0]), :] = embed_in_ref[...]
    down_ref[...] = jnp.zeros_like(down_ref)

    packs.arrive()
    coarse_setup(lat, lon, nb_ref, cells_ref, rowmix_ref, colmix_ref)
    lift(embed_ref, cells_ref, rowmix_ref, colmix_ref, mid_ref, l3_ref)
    edges.arrive()
    close_edges(lat, cot_ref, rowhalo_ref, colhalo_ref, c3_ref)
    back_around(c3_ref, w2t_ref, back_ref)
    middle(lat, 0, 9, l3_ref, back_ref, w1_ref, h3_ref, d3_ref)
    middle(lat, 9, 8, l3_ref, back_ref, w1_ref, h3_ref, d3_ref)

    weight_grad(h3_ref, 0, c3_ref, 2, part2)
    sum2.step_pair()
    weight_grad(l3_ref, 1, d3_ref, 1, part1)
    sum1.step_pair()
    sum2.step_scatter()
    back_to_embed(0, 8, d3_ref, w1t_ref, cot_ref, rowmix_ref, colmix_ref, down_ref)
    sum1.step_scatter()
    back_to_embed(8, 8, d3_ref, w1t_ref, cot_ref, rowmix_ref, colmix_ref, down_ref)
    embed_grad(cells_ref, down_ref, eparts.at[0])
    small.begin(0)
    features_of(0, 8, h3_ref, l3_ref, w2_ref, feat_ref)
    small.pass_on(0)
    sum2.step_column()
    features_of(8, 8, h3_ref, l3_ref, w2_ref, feat_ref)
    sum1.step_column()
    small.pass_on(1)
    sum2.step_gather()
    sum1.step_gather()
    small.finish(gemb_ref, scale)
    sum2.step_swap(g2_ref, scale)
    sum1.step_swap(g1_ref, scale)
    sum2.finish(g2_ref, scale)
    sum1.finish(g1_ref, scale)
    packs.sent()
    edges.sent()


def scratch_list(channels=73):
    dma = pltpu.SemaphoreType.DMA
    line = lambda n, kind: pltpu.VMEM((1, n), kind)
    tiles = lambda *n: pltpu.VMEM((*n, 16, HID), BF)
    grad = [
        tiles(TILES), tiles(HALF), tiles(16 * PIECE), tiles(15, PIECE),
        tiles(PIECE), tiles(3, PIECE), tiles(16 * PIECE), tiles(HALF),
    ]
    return (
        [
            pltpu.VMEM((CELLS, channels), BF),
            line(ROWS, jnp.int32), line(ROWS, F32), line(COLS, jnp.int32), line(COLS, F32),
            pltpu.VMEM((channels, HID), BF),
            pltpu.VMEM((3, 3, HID, HID), BF),
            pltpu.VMEM((3, 3, HID, HID), BF),
            pltpu.VMEM((ROWS, COLS, HID), BF),
            pltpu.VMEM((16, HID), F32),
            pltpu.VMEM((PACK, HID), BF),
            pltpu.VMEM((HID, HID), BF),
            pltpu.VMEM((9, PACK, HID), BF),
            pltpu.VMEM((2, 2, COLS, HID), BF),
            pltpu.VMEM((2, ROWS + 4, 16, HID), BF),
            pltpu.VMEM((12, 24, HID), F32),
            pltpu.VMEM((8, HID), F32),
            pltpu.VMEM((64, 2 * HID), BF),
            pltpu.VMEM((WIDE, NUM_J * HID), F32),
            pltpu.VMEM((12, 32, HID), F32),
        ]
        + [pltpu.VMEM((12 * HID, 2 * HID), BF)] * 4
        + [pltpu.VMEM((18, 2, WIDE, 3 * HID), BF)] * 2
        + [pltpu.VMEM((17, 2, WIDE, 3 * HID), BF)] * 2
        + [pltpu.VMEM((17, WIDE, 2 * HID), F32)]
        + grad
        + grad
        + [tiles(3, EMBED_TILES), tiles(19, EMBED_TILES)]
        + [dma((9,))]
        + [dma((8,))] * 4
        + [dma((4,)), dma((15,)), dma((15,)), dma((3,)), dma((3,)), dma((15,)), dma((15,))] * 2
        + [dma((19,))] * 2
    )


def on_device(coarse, row_src, row_frac, col_src, col_frac, embed_weight, conv1_weight, conv2_weight, cotangent):
    channels = coarse.shape[0]
    cells = jnp.transpose(coarse, (1, 2, 0)).reshape(CELLS, channels)
    lines = [v.reshape(1, -1) for v in (row_src, row_frac, col_src, col_frac)]
    features, grad_embed, grad_conv1, grad_conv2 = pl.pallas_call(
        kernel,
        out_shape=[
            pltpu.VMEM((ROWS, COLS, HID), BF),
            pltpu.VMEM((EMBED_TILES * 16, HID), F32),
            pltpu.VMEM((TILES, 16, HID), F32),
            pltpu.VMEM((TILES, 16, HID), F32),
        ],
        in_specs=[pl.BlockSpec(memory_space=pl.ANY)] * 9,
        out_specs=[pl.BlockSpec(memory_space=pltpu.VMEM)] * 4,
        scratch_shapes=scratch_list(channels),
        compiler_params=pltpu.CompilerParams(
            collective_id=0, has_side_effects=True, vmem_limit_bytes=56 * 2**20
        ),
    )(cells, *lines, embed_weight, conv1_weight, conv2_weight, cotangent)
    taps = (3, 3, HID, HID)
    return (features, grad_embed[:channels], grad_conv1.reshape(taps), grad_conv2.reshape(taps))


def solution(mesh):
    in_specs = (
        P(None, "lat", "lon"),
        P("lat"),
        P("lat"),
        P("lon"),
        P("lon"),
        P(),
        P(),
        P(),
        P("lat", "lon", None),
    )
    out_specs = (P("lat", "lon", None), P(), P(), P())
    return jax.shard_map(
        on_device, mesh=mesh, in_specs=in_specs, out_specs=out_specs, check_vma=False
    )
```

time: 68.7 us -> 55.6 us (0.81)
  local copies, waits for them, and re-layouts: 10.2 us -> 3.22 us
  Pallas kernels: 57.5 us -> 51.7 us
    pallas_call x1, Pallas kernels: 57.5 us -> 51.7 us  [on_device(): pl.pallas_call(kernel, out_shape=[pltpu.VMEM((ROWS, COLS, HID), BF), pltp...]
    unnamed x22 -> x4, local copies, waits for them, and re-layouts: 7.72 us -> 3.22 us
    concatenate x1 -> x0, local copies, waits for them, and re-layouts: 1.79 us -> none  [pack_block(): return jnp.concatenate([cells, lines], axis=0)]
where the time goes in v2:
time: 55.6 us; the launch traced here: 55.5 us
  Pallas kernels  51.7 us (93%)
  local copies, waits for them, and re-layouts  3.22 us (6%)
  between operations  0.64 us (1%)
    pallas_call x1, Pallas kernels, on_device(): pl.pallas_call(kernel, out_shape=[pltpu.VMEM((ROWS, COLS, HID), BF), pltp...  51.7 us
    unnamed x4, local copies, waits for them, and re-layouts  3.22 us

profile of v2, /device:TPU:1, one launch (start us, length us, event | category | flops | bytes accessed | tf_op | source)
XLA Modules:
  0.0 55.5 jit_solution(3183730847167493581)
XLA Ops:
  0.6 51.7 %shard_map.120 = (bf16[32,128,128]{2,1,0:T(8,128)(2,1)S(1)}, f32[80,128]{1,0:T(8,128)S(1)}, f32[72,16,128]{2,1,0:T(8,128)S(1)}, f32[72,16,128]{2,1,0:T(8,128)S(1)}) custom-call(bf16[32,73]{1,0:T(8,128)(2,1)} %bitcast.13, s32[1,32]{1,0:T(1,128)} %bitcast.14, f32[1,32]{1,0:T(1,128)} %bitcast.15, s32[1,128]{1,0:T(1,128)} %bitcast.16, f32[1,128]{1,0:T(1,128)} %bitcast.17, ...), custom_call_target="tpu_custom_call" | custom-call | tf_op jit(solution)/shard_map/pallas_call | solution.py:583
  52.3 1.0 %copy.17 = bf16[32,128,128]{2,1,0:T(8,128)(2,1)} copy(bf16[32,128,128]{2,1,0:T(8,128)(2,1)S(1)} %get-tuple-element.12) | data formatting | bytes 2097152
  53.3 0.8 %copy.18 = f32[3,3,128,128]{3,2,1,0:T(8,128)} copy(f32[3,3,128,128]{3,2,1,0:T(8,128)S(1)} %bitcast.11) | data formatting | bytes 1179648
  54.1 0.8 %copy.19 = f32[3,3,128,128]{3,2,1,0:T(8,128)} copy(f32[3,3,128,128]{3,2,1,0:T(8,128)S(1)} %bitcast.10) | data formatting | bytes 1179648
  54.9 0.6 %copy.20 = f32[73,128]{1,0:T(8,128)} copy(f32[73,128]{1,0:T(8,128)S(1)} %bitcast.12) | data formatting | bytes 74752

commit v3 on v2

--- a/solution.py
+++ b/solution.py
@@ -150,36 +150,56 @@
     lax.fori_loop(0, ROWS // 2, step, 0)
 
 
-def close_edges(lat, cot_ref, rowhalo_ref, colhalo_ref, c3_ref):
+def gather_columns(cot_ref, colpack_ref):
+    spot = lax.broadcasted_iota(jnp.int32, (16, HID), 0) // 2
+    for side, start in ((0, 0), (1, COLS - 16)):
+        for g in range(ROWS // 8):
+            total = None
+            for n in range(8):
+                x = cot_ref[8 * g + n, pl.ds(start, 16)].astype(F32)
+                shift = (2 * n + 2 * side) % 16
+                x = pltpu.roll(x, shift, 0) if shift else x
+                total = x if n == 0 else jnp.where(spot == n, x, total)
+            colpack_ref[side, g] = total.astype(BF)
+
+
+def beside(colhalo_ref, tile, n):
     near = lax.broadcasted_iota(jnp.int32, (16, HID), 0) < 8
-
-    def beside(i):
-        return jnp.where(near, colhalo_ref[1, i].astype(F32), colhalo_ref[0, i].astype(F32))
-
+    right = colhalo_ref[1, tile].astype(F32)
+    left = colhalo_ref[0, tile].astype(F32)
+    right = pltpu.roll(right, 16 - 2 * n, 0) if n else right
+    left = pltpu.roll(left, 14 - 2 * n, 0) if n < 7 else left
+    return jnp.where(near, right, left)
+
+
+def close_columns(cot_ref, colhalo_ref, c3_ref):
+    def step(g, carry):
+        for n in range(8):
+            r = 8 * g + n
+            last = cot_ref[r, pl.ds(COLS - 16, 16)].astype(F32)
+            first = cot_ref[r, pl.ds(0, 16)].astype(F32)
+            x = jnp.concatenate([last, beside(colhalo_ref, g, n), first], axis=0)
+            west = pltpu.roll(x, 1, 0).astype(BF)
+            east = pltpu.roll(x, 47, 0).astype(BF)
+            wide = pl.ds(COLS, 16)
+            q, t = 4 * g + n // 2 + 1, n % 2
+            c3_ref[q, t, wide, pl.ds(HID, HID)] = x[16:32].astype(BF)
+            c3_ref[q, t, wide, pl.ds(0, HID)] = west[16:32]
+            c3_ref[q, t, pl.ds(0, 16), pl.ds(0, HID)] = west[32:48]
+            c3_ref[q, t, pl.ds(COLS - 16, 32), pl.ds(2 * HID, HID)] = east[0:32]
+        return carry
+
+    lax.fori_loop(0, ROWS // 8, step, 0)
+
+
+def close_rows(lat, rowhalo_ref, colhalo_ref, c3_ref):
     top = (lat > 0).astype(F32)
     bottom = (lat < 7).astype(F32)
     for t in range(2):
-        x = jnp.concatenate([rowhalo_ref[0, t].astype(F32), beside(t)], axis=0)
+        x = jnp.concatenate([rowhalo_ref[0, t].astype(F32), beside(colhalo_ref, 4, 6 + t)], axis=0)
         store_shifted(c3_ref, 0, t, x * top)
-        x = jnp.concatenate([rowhalo_ref[1, t].astype(F32), beside(ROWS + 2 + t)], axis=0)
+        x = jnp.concatenate([rowhalo_ref[1, t].astype(F32), beside(colhalo_ref, 5, t)], axis=0)
         store_shifted(c3_ref, 17, t, x * bottom)
-
-    def step(q, carry):
-        for t in range(2):
-            r = 2 * q + t
-            last = cot_ref[r, pl.ds(COLS - 16, 16)].astype(F32)
-            first = cot_ref[r, pl.ds(0, 16)].astype(F32)
-            x = jnp.concatenate([last, beside(r + 2), first], axis=0)
-            west = pltpu.roll(x, 1, 0).astype(BF)
-            east = pltpu.roll(x, 47, 0).astype(BF)
-            wide = pl.ds(COLS, 16)
-            c3_ref[q + 1, t, wide, pl.ds(HID, HID)] = x[16:32].astype(BF)
-            c3_ref[q + 1, t, wide, pl.ds(0, HID)] = west[16:32]
-            c3_ref[q + 1, t, pl.ds(0, 16), pl.ds(0, HID)] = west[32:48]
-            c3_ref[q + 1, t, pl.ds(COLS - 16, 32), pl.ds(2 * HID, HID)] = east[0:32]
-        return carry
-
-    lax.fori_loop(0, ROWS // 2, step, 0)
 
 
 def back_inside(c3_ref, w2t_ref, back_ref):
@@ -201,23 +221,52 @@
     back_ref[16] = y[720 + WIDE : 720 + 2 * WIDE]
 
 
-def middle(lat, first, count, l3_ref, back_ref, w1_ref, h3_ref, d3_ref):
-    pre_all = dot(four_rows(l3_ref, first, count, WIDE), w1_ref[...])
-    top = (lat > 0).astype(F32)
-    bottom = (lat < 7).astype(F32)
-    for p in range(count):
+def make_hidden(lat, l3_ref, w1_ref, h3_ref, slope_ref):
+    def finish(pre_all, first, count):
+        for p in range(count):
+            for s in range(2):
+                pre = pre_all[p * WIDE : (p + 1) * WIDE, s * HID : (s + 1) * HID]
+                sig = 0.5 + 0.5 * jnp.tanh(0.5 * pre)
+                hidden = pre * sig
+                slope = sig + hidden * (1.0 - sig)
+                if first + p == 0 and s == 0:
+                    inside = (lat > 0).astype(F32)
+                    hidden, slope = hidden * inside, slope * inside
+                if first + p == 16 and s == 1:
+                    inside = (lat < 7).astype(F32)
+                    hidden, slope = hidden * inside, slope * inside
+                h3_ref[first + p, s, :, pl.ds(HID, HID)] = hidden.astype(BF)
+                slope_ref[first + p, :, pl.ds(s * HID, HID)] = slope
+
+    waiting = None
+    for first in range(0, 17, 3):
+        count = min(3, 17 - first)
+        pre_all = dot(four_rows(l3_ref, first, count, WIDE), w1_ref[...])
+        if waiting is not None:
+            finish(*waiting)
+        waiting = (pre_all, first, count)
+    finish(*waiting)
+
+
+def shift_hidden(h3_ref):
+    def step(p, carry):
         for s in range(2):
-            pre = pre_all[p * WIDE : (p + 1) * WIDE, s * HID : (s + 1) * HID]
-            back = back_ref[first + p, :, pl.ds(s * HID, HID)]
-            sig = 0.5 + 0.5 * jnp.tanh(0.5 * pre)
-            hidden = pre * sig
-            delta = back * (sig + hidden * (1.0 - sig))
-            if first + p == 0 and s == 0:
-                hidden, delta = hidden * top, delta * top
-            if first + p == 16 and s == 1:
-                hidden, delta = hidden * bottom, delta * bottom
-            store_shifted(h3_ref, first + p, s, hidden)
-            store_shifted(d3_ref, first + p, s, delta)
+            x = h3_ref[p, s, :, pl.ds(HID, HID)].astype(F32)
+            h3_ref[p, s, :, pl.ds(0, HID)] = pltpu.roll(x, 1, 0).astype(BF)
+            h3_ref[p, s, :, pl.ds(2 * HID, HID)] = pltpu.roll(x, WIDE - 1, 0).astype(BF)
+        return carry
+
+    lax.fori_loop(0, 17, step, 0)
+
+
+def make_delta(back_ref, slope_ref, d3_ref):
+    def step(p, carry):
+        for s in range(2):
+            lanes = pl.ds(s * HID, HID)
+            store_shifted(d3_ref, p, s, back_ref[p, :, lanes] * slope_ref[p, :, lanes])
+        return carry
+
+    lax.fori_loop(0, 17, step, 0)
 
 
 def rows_from(ref, start, lanes):
@@ -296,25 +345,24 @@
 
 
 class Exchange:
-    def __init__(self, copies):
+    def __init__(self, copies, span, sems):
         self.copies = copies
+        self.whole = [pltpu.make_async_copy(span, span, sem) for sem in sems]
 
     def start(self):
         for c in self.copies:
             c.start()
 
     def arrive(self):
-        for c in self.copies:
-            c.wait_recv()
+        self.whole[1].wait()
 
     def sent(self):
-        for c in self.copies:
-            c.wait_send()
-
-
-def remote(src, dst, send, recv, target):
+        self.whole[0].wait()
+
+
+def remote(src, dst, sems, target):
     return pltpu.make_async_remote_copy(
-        src_ref=src, dst_ref=dst, send_sem=send, recv_sem=recv, device_id=target, device_id_type=MESH
+        src_ref=src, dst_ref=dst, send_sem=sems[0], recv_sem=sems[1], device_id=target, device_id_type=MESH
     )
 
 
@@ -322,27 +370,28 @@
     def __init__(self, place, part, paired, half, got, mine, other, final, twin, sems):
         self.part, self.paired, self.half, self.got = part, paired, half, got
         self.mine, self.other, self.final, self.twin = mine, other, final, twin
-        a_sem, s_send, s_recv, z_send, z_recv, g_send, g_recv = sems
+        pairs = [(sems.at[2 * n], sems.at[2 * n + 1]) for n in range(5)]
         self.keep = place.core * HALF
         self.own = pl.ds(place.plane * PIECE, PIECE)
         away = part.at[pl.ds(HALF - self.keep, HALF)]
-        self.pair = Exchange([remote(away, paired, a_sem.at[0], a_sem.at[1], place.mate)])
+        self.pair = Exchange([remote(away, paired, pairs[0], place.mate)], paired, pairs[0])
         self.scatter = Exchange(
             [
-                remote(half.at[pl.ds(q * PIECE, PIECE)], got.at[n], s_send.at[n], s_recv.at[n], t)
+                remote(half.at[pl.ds(q * PIECE, PIECE)], got.at[n], pairs[1], t)
                 for n, (q, t) in enumerate(zip(place.planes, place.plane_mates))
-            ]
+            ],
+            got,
+            pairs[1],
         )
         self.column = Exchange(
-            [remote(mine, other.at[n], z_send.at[n], z_recv.at[n], t) for n, t in enumerate(place.z_mates)]
+            [remote(mine, other.at[n], pairs[2], t) for n, t in enumerate(place.z_mates)], other, pairs[2]
         )
         self.gather = Exchange(
-            [
-                remote(final.at[self.own], final.at[self.own], g_send.at[n], g_recv.at[n], t)
-                for n, t in enumerate(place.plane_mates)
-            ]
+            [remote(final.at[self.own], final.at[self.own], pairs[3], t) for t in place.plane_mates],
+            final.at[pl.ds(0, 15 * PIECE)],
+            pairs[3],
         )
-        self.swap = Exchange([remote(final.at[pl.ds(0, HALF)], twin, a_sem.at[2], a_sem.at[3], place.mate)])
+        self.swap = Exchange([remote(final.at[pl.ds(0, HALF)], twin, pairs[4], place.mate)], twin, pairs[4])
 
     def step_pair(self):
         self.pair.start()
@@ -370,47 +419,63 @@
         self.final[self.own] = total.astype(BF)
         self.gather.start()
 
-    def step_swap(self, out_ref, scale):
+    def step_swap(self, full_ref, out_ref, sem, scale):
         self.gather.arrive()
         self.swap.start()
-        out_ref[pl.ds(self.keep, HALF)] = self.final[pl.ds(0, HALF)].astype(F32) * scale
-
-    def finish(self, out_ref, scale):
+        self.outs = [
+            pltpu.make_async_copy(full_ref.at[part], out_ref.at[part], sem.at[n])
+            for n, part in enumerate((pl.ds(self.keep, HALF), pl.ds(HALF - self.keep, HALF)))
+        ]
+        full_ref[pl.ds(self.keep, HALF)] = self.final[pl.ds(0, HALF)].astype(F32) * scale
+        self.outs[0].start()
+
+    def finish(self, full_ref, scale):
         self.swap.arrive()
-        out_ref[pl.ds(HALF - self.keep, HALF)] = self.twin[...].astype(F32) * scale
+        full_ref[pl.ds(HALF - self.keep, HALF)] = self.twin[...].astype(F32) * scale
+        self.outs[1].start()
+
+    def drain(self):
         for e in (self.pair, self.scatter, self.column, self.gather, self.swap):
             e.sent()
+        for out in self.outs:
+            out.wait()
 
 
 class SmallSum:
     def __init__(self, place, parts, slots, sems):
         self.parts, self.slots = parts, slots
+        self.keep = pl.ds(place.core * 2, 3)
+        self.away = pl.ds(2 - place.core * 2, 3)
         self.steps = []
         base = 0
-        for g, targets in enumerate([[place.mate], place.z_mates, place.plane_mates]):
+        for g, targets in enumerate([[place.mate], place.z_mates, place.plane_mates, [place.mate]]):
+            size = EMBED_TILES if g == 0 else 3
+            pair = (sems.at[2 * g], sems.at[2 * g + 1])
             copies = []
-            for n, t in enumerate(targets):
-                copies.append(remote(parts.at[g], slots.at[base + n], sems[0].at[base + n], sems[1].at[base + n], t))
-            self.steps.append((base, len(targets), Exchange(copies)))
+            for n, t in enumerate(targets, base):
+                copies.append(remote(parts.at[g, pl.ds(0, size)], slots.at[n, pl.ds(0, size)], pair, t))
+            span = slots.at[pl.ds(base, len(targets)), pl.ds(0, size)]
+            self.steps.append((base, len(targets), Exchange(copies, span, pair)))
             base += len(targets)
 
-    def begin(self, g):
-        self.steps[g][2].start()
-
-    def total(self, g):
+    def begin(self):
+        self.steps[0][2].start()
+
+    def pass_on(self, g):
         base, count, exchange = self.steps[g]
         exchange.arrive()
-        total = self.parts[g].astype(F32)
+        here = self.keep if g == 0 else pl.ds(0, 3)
+        total = self.parts[g, here].astype(F32)
         for n in range(count):
-            total = total + self.slots[base + n].astype(F32)
-        return total
-
-    def pass_on(self, g):
-        self.parts[g + 1] = self.total(g).astype(BF)
-        self.begin(g + 1)
+            total = total + self.slots[base + n, here].astype(F32)
+        self.parts[g + 1, pl.ds(0, 3)] = total.astype(BF)
+        self.steps[g + 1][2].start()
 
     def finish(self, out_ref, scale):
-        out_ref[...] = (self.total(2) * scale).reshape(EMBED_TILES * 16, HID)
+        base, _, exchange = self.steps[3]
+        exchange.arrive()
+        out_ref[self.away] = self.slots[base, pl.ds(0, 3)].astype(F32) * scale
+        out_ref[self.keep] = self.parts[3, pl.ds(0, 3)].astype(F32) * scale
         for _, _, exchange in self.steps:
             exchange.sent()
 
@@ -432,18 +497,24 @@
 
 def kernel(
     coarse_hbm, row_src_hbm, row_frac_hbm, col_src_hbm, col_frac_hbm, embed_hbm, conv1_hbm, conv2_hbm, cot_hbm,
-    feat_ref, gemb_ref, g1_ref, g2_ref,
+    feat_out, gemb_out, g1_out, g2_out,
+    feat_ref, gemb_ref, g1_ref, g2_ref, out_sem,
     coarse_ref, row_src_ref, row_frac_ref, col_src_ref, col_frac_ref, embed_in_ref, conv1_ref, conv2_ref, cot_ref,
     lines_ref, pack_ref, embed_ref,
-    nb_ref, rowhalo_ref, colhalo_ref, cells_ref, rowmix_ref, colmix_ref, mid_ref, down_ref,
-    w1_ref, w2_ref, w1t_ref, w2t_ref, l3_ref, c3_ref, h3_ref, d3_ref, back_ref,
+    nb_ref, rowhalo_ref, colpack_ref, colhalo_ref, cells_ref, rowmix_ref, colmix_ref, mid_ref, down_ref,
+    w1_ref, w2_ref, w1t_ref, w2t_ref, l3_ref, c3_ref, h3_ref, d3_ref, back_ref, slope_ref,
     part1, paired1, half1, got1, mine1, other1, final1, twin1,
     part2, paired2, half2, got2, mine2, other2, final2, twin2, eparts, eslots,
-    load_sem, halo_send, halo_recv, cot_send, cot_recv, *sems,
+    load_sem, halo_sem, sum_sem,
 ):
     place = Place()
     lat, lon = place.lat, place.lon
     scale = 1.0 / math.sqrt(8 * ROWS * 16 * COLS)
+
+    def apart(stage, *args):
+        @pl.when(lat < 8)
+        def _():
+            stage(*args)
 
     barrier = pltpu.get_barrier_semaphore()
     partners = [place.mate] + place.around + place.z_mates + place.plane_mates
@@ -459,23 +530,29 @@
     for load in loads:
         load.start()
 
-    packs, edges = [], []
+    packs, columns, rows, corners = [], [], [], []
+    pairs = [(halo_sem.at[2 * n], halo_sem.at[2 * n + 1]) for n in range(4)]
     for n, (dy, dx) in enumerate(DIRS):
         slot = (1 - dy) * 3 + 1 - dx
-        packs.append(remote(pack_ref, nb_ref.at[slot], halo_send.at[n], halo_recv.at[n], place.around[n]))
-        rows = {-1: pl.ds(0, 2), 0: pl.ds(0, ROWS), 1: pl.ds(ROWS - 2, 2)}[dy]
+        packs.append(remote(pack_ref, nb_ref.at[slot], pairs[0], place.around[n]))
         if dx == 0:
-            src = cot_ref.at[rows]
-            dst = rowhalo_ref.at[0 if dy == 1 else 1]
+            src = cot_ref.at[pl.ds(0 if dy == -1 else ROWS - 2, 2)]
+            rows.append(remote(src, rowhalo_ref.at[0 if dy == 1 else 1], pairs[2], place.around[n]))
         else:
-            src = cot_ref.at[rows, pl.ds(0 if dx == -1 else COLS - 16, 16)]
-            land = {1: pl.ds(0, 2), 0: pl.ds(2, ROWS), -1: pl.ds(ROWS + 2, 2)}[dy]
-            dst = colhalo_ref.at[1 if dx == -1 else 0, land]
-        edges.append(remote(src, dst, cot_send.at[n], cot_recv.at[n], place.around[n]))
-    packs, edges = Exchange(packs), Exchange(edges)
-    sum1 = GradSum(place, part1, paired1, half1, got1, mine1, other1, final1, twin1, sems[0:7])
-    sum2 = GradSum(place, part2, paired2, half2, got2, mine2, other2, final2, twin2, sems[7:14])
-    small = SmallSum(place, eparts, eslots, sems[14:16])
+            side = 0 if dx == -1 else 1
+            src = colpack_ref.at[side, {-1: pl.ds(0, 1), 0: pl.ds(0, 4), 1: pl.ds(3, 1)}[dy]]
+            dst = colhalo_ref.at[1 - side, {1: pl.ds(4, 1), 0: pl.ds(0, 4), -1: pl.ds(5, 1)}[dy]]
+            if dy == 0:
+                columns.append(remote(src, dst, pairs[1], place.around[n]))
+            else:
+                corners.append(remote(src, dst, pairs[3], place.around[n]))
+    packs = Exchange(packs, nb_ref.at[pl.ds(0, 8)], pairs[0])
+    columns = Exchange(columns, colhalo_ref.at[:, pl.ds(0, 4)], pairs[1])
+    rows = Exchange(rows, rowhalo_ref, pairs[2])
+    corners = Exchange(corners, colhalo_ref.at[:, pl.ds(4, 2)], pairs[3])
+    sum1 = GradSum(place, part1, paired1, half1, got1, mine1, other1, final1, twin1, sum_sem.at[pl.ds(0, 10)])
+    sum2 = GradSum(place, part2, paired2, half2, got2, mine2, other2, final2, twin2, sum_sem.at[pl.ds(10, 10)])
+    small = SmallSum(place, eparts, eslots, sum_sem.at[pl.ds(20, 8)])
 
     for load in loads[0:5]:
         load.wait()
@@ -483,14 +560,15 @@
     loads[5].wait()
     pl.semaphore_wait(barrier, len(partners))
     packs.start()
-    edges.start()
+    gather_columns(cot_ref, colpack_ref)
+    columns.start()
 
     nb_ref[4] = pack_ref[...]
     for load in loads[6:9]:
         load.wait()
     spread_taps(conv2_ref, w2t_ref, True)
     spread_own(cot_ref, c3_ref)
-    back_inside(c3_ref, w2t_ref, back_ref)
+    apart(back_inside, c3_ref, w2t_ref, back_ref)
     spread_taps(conv1_ref, w1_ref, False)
     spread_taps(conv2_ref, w2_ref, False)
     spread_taps(conv1_ref, w1t_ref, True)
@@ -499,39 +577,74 @@
     down_ref[...] = jnp.zeros_like(down_ref)
 
     packs.arrive()
+    corners.start()
+    rows.start()
     coarse_setup(lat, lon, nb_ref, cells_ref, rowmix_ref, colmix_ref)
     lift(embed_ref, cells_ref, rowmix_ref, colmix_ref, mid_ref, l3_ref)
-    edges.arrive()
-    close_edges(lat, cot_ref, rowhalo_ref, colhalo_ref, c3_ref)
-    back_around(c3_ref, w2t_ref, back_ref)
-    middle(lat, 0, 9, l3_ref, back_ref, w1_ref, h3_ref, d3_ref)
-    middle(lat, 9, 8, l3_ref, back_ref, w1_ref, h3_ref, d3_ref)
-
-    weight_grad(h3_ref, 0, c3_ref, 2, part2)
+    apart(make_hidden, lat, l3_ref, w1_ref, h3_ref, slope_ref)
+    columns.arrive()
+    close_columns(cot_ref, colhalo_ref, c3_ref)
+    apart(weight_grad, h3_ref, 0, c3_ref, 2, part2)
     sum2.step_pair()
-    weight_grad(l3_ref, 1, d3_ref, 1, part1)
+    corners.arrive()
+    rows.arrive()
+    close_rows(lat, rowhalo_ref, colhalo_ref, c3_ref)
+    apart(back_around, c3_ref, w2t_ref, back_ref)
+    sum2.step_scatter()
+    make_delta(back_ref, slope_ref, d3_ref)
+    apart(weight_grad, l3_ref, 1, d3_ref, 1, part1)
     sum1.step_pair()
-    sum2.step_scatter()
-    back_to_embed(0, 8, d3_ref, w1t_ref, cot_ref, rowmix_ref, colmix_ref, down_ref)
+    apart(back_to_embed, 0, 8, d3_ref, w1t_ref, cot_ref, rowmix_ref, colmix_ref, down_ref)
     sum1.step_scatter()
-    back_to_embed(8, 8, d3_ref, w1t_ref, cot_ref, rowmix_ref, colmix_ref, down_ref)
+    apart(back_to_embed, 8, 8, d3_ref, w1t_ref, cot_ref, rowmix_ref, colmix_ref, down_ref)
     embed_grad(cells_ref, down_ref, eparts.at[0])
-    small.begin(0)
-    features_of(0, 8, h3_ref, l3_ref, w2_ref, feat_ref)
+    small.begin()
+    sum2.step_column()
+    shift_hidden(h3_ref)
     small.pass_on(0)
-    sum2.step_column()
-    features_of(8, 8, h3_ref, l3_ref, w2_ref, feat_ref)
+    done = [
+        pltpu.make_async_copy(feat_ref.at[pl.ds(n * 16, 16)], feat_out.at[pl.ds(n * 16, 16)], out_sem.at[n])
+        for n in range(2)
+    ]
+    apart(features_of, 0, 8, h3_ref, l3_ref, w2_ref, feat_ref)
+    done[0].start()
+    apart(features_of, 8, 8, h3_ref, l3_ref, w2_ref, feat_ref)
+    done[1].start()
+    sum2.step_gather()
     sum1.step_column()
     small.pass_on(1)
-    sum2.step_gather()
     sum1.step_gather()
+    sum2.step_swap(g2_ref, g2_out, out_sem.at[pl.ds(2, 2)], scale)
+    small.pass_on(2)
+    sum2.finish(g2_ref, scale)
     small.finish(gemb_ref, scale)
-    sum2.step_swap(g2_ref, scale)
-    sum1.step_swap(g1_ref, scale)
-    sum2.finish(g2_ref, scale)
+    done.append(pltpu.make_async_copy(gemb_ref, gemb_out, out_sem.at[4]))
+    done[2].start()
+    sum1.step_swap(g1_ref, g1_out, out_sem.at[pl.ds(5, 2)], scale)
     sum1.finish(g1_ref, scale)
-    packs.sent()
-    edges.sent()
+    for exchange in (packs, columns, rows, corners):
+        exchange.sent()
+    for copy in done:
+        copy.wait()
+    sum2.drain()
+    sum1.drain()
+
+
+def write_out(*refs):
+    count = (len(refs) - 1) // 2
+    copies = [pltpu.make_async_copy(refs[n], refs[count + n], refs[-1].at[n]) for n in range(count)]
+    for copy in copies:
+        copy.start()
+    for copy in copies:
+        copy.wait()
+
+
+RESULTS = [
+    ((ROWS, COLS, HID), BF),
+    ((EMBED_TILES, 16, HID), F32),
+    ((TILES, 16, HID), F32),
+    ((TILES, 16, HID), F32),
+]
 
 
 def scratch_list(channels=73):
@@ -543,7 +656,9 @@
         tiles(PIECE), tiles(3, PIECE), tiles(16 * PIECE), tiles(HALF),
     ]
     return (
-        [
+        [pltpu.VMEM(shape, kind) for shape, kind in RESULTS]
+        + [dma((7,))]
+        + [
             pltpu.VMEM((CELLS, channels), BF),
             line(ROWS, jnp.int32), line(ROWS, F32), line(COLS, jnp.int32), line(COLS, F32),
             pltpu.VMEM((channels, HID), BF),
@@ -555,7 +670,8 @@
             pltpu.VMEM((HID, HID), BF),
             pltpu.VMEM((9, PACK, HID), BF),
             pltpu.VMEM((2, 2, COLS, HID), BF),
-            pltpu.VMEM((2, ROWS + 4, 16, HID), BF),
+            tiles(2, 4),
+            tiles(2, 6),
             pltpu.VMEM((12, 24, HID), F32),
             pltpu.VMEM((8, HID), F32),
             pltpu.VMEM((64, 2 * HID), BF),
@@ -565,14 +681,12 @@
         + [pltpu.VMEM((12 * HID, 2 * HID), BF)] * 4
         + [pltpu.VMEM((18, 2, WIDE, 3 * HID), BF)] * 2
         + [pltpu.VMEM((17, 2, WIDE, 3 * HID), BF)] * 2
-        + [pltpu.VMEM((17, WIDE, 2 * HID), F32)]
+        + [pltpu.VMEM((17, WIDE, 2 * HID), F32)] * 2
         + grad
         + grad
-        + [tiles(3, EMBED_TILES), tiles(19, EMBED_TILES)]
+        + [tiles(4, EMBED_TILES), tiles(20, EMBED_TILES)]
         + [dma((9,))]
-        + [dma((8,))] * 4
-        + [dma((4,)), dma((15,)), dma((15,)), dma((3,)), dma((3,)), dma((15,)), dma((15,))] * 2
-        + [dma((19,))] * 2
+        + [dma((8,)), dma((28,))]
     )
 
 
@@ -580,23 +694,26 @@
     channels = coarse.shape[0]
     cells = jnp.transpose(coarse, (1, 2, 0)).reshape(CELLS, channels)
     lines = [v.reshape(1, -1) for v in (row_src, row_frac, col_src, col_frac)]
-    features, grad_embed, grad_conv1, grad_conv2 = pl.pallas_call(
+    results = pl.pallas_call(
         kernel,
-        out_shape=[
-            pltpu.VMEM((ROWS, COLS, HID), BF),
-            pltpu.VMEM((EMBED_TILES * 16, HID), F32),
-            pltpu.VMEM((TILES, 16, HID), F32),
-            pltpu.VMEM((TILES, 16, HID), F32),
-        ],
+        out_shape=[pltpu.VMEM(shape, kind) for shape, kind in RESULTS],
         in_specs=[pl.BlockSpec(memory_space=pl.ANY)] * 9,
-        out_specs=[pl.BlockSpec(memory_space=pltpu.VMEM)] * 4,
+        out_specs=[pl.BlockSpec(memory_space=pl.ANY)] * 4,
         scratch_shapes=scratch_list(channels),
         compiler_params=pltpu.CompilerParams(
             collective_id=0, has_side_effects=True, vmem_limit_bytes=56 * 2**20
         ),
     )(cells, *lines, embed_weight, conv1_weight, conv2_weight, cotangent)
+    features, grad_embed, grad_conv1, grad_conv2 = pl.pallas_call(
+        write_out,
+        out_shape=[jax.ShapeDtypeStruct(shape, kind) for shape, kind in RESULTS],
+        in_specs=[pl.BlockSpec(memory_space=pl.ANY)] * 4,
+        out_specs=[pl.BlockSpec(memory_space=pl.ANY)] * 4,
+        scratch_shapes=[pltpu.SemaphoreType.DMA((4,))],
+    )(*[pltpu.with_memory_space_constraint(r, pltpu.VMEM) for r in results])
     taps = (3, 3, HID, HID)
-    return (features, grad_embed[:channels], grad_conv1.reshape(taps), grad_conv2.reshape(taps))
+    grad_embed = grad_embed.reshape(EMBED_TILES * 16, HID)[:channels]
+    return (features, grad_embed, grad_conv1.reshape(taps), grad_conv2.reshape(taps))
 
 
 def solution(mesh):

time: 55.6 us -> 43.5 us (0.78)
  Pallas kernels: 51.7 us -> 42.7 us
  local copies, waits for them, and re-layouts: 3.22 us -> 0 us
    pallas_call x1 -> x2, Pallas kernels: 51.7 us -> 42.7 us  [the longest x1 41.3 us: on_device(): pl.pallas_call(kernel, out_shape=[pltpu.VMEM(shape, kind) for shape, kind...]
    unnamed x4 -> x0, local copies, waits for them, and re-layouts: 3.22 us -> none
where the time goes in v3:
time: 43.5 us; the launch traced here: 43.4 us
  Pallas kernels  42.7 us (98%)
  between operations  0.64 us (1%)
    pallas_call x1, Pallas kernels, on_device(): pl.pallas_call(kernel, out_shape=[pltpu.VMEM(shape, kind) for shape, kind...  41.3 us
    pallas_call x1, Pallas kernels, on_device(): pl.pallas_call(write_out, out_shape=[jax.ShapeDtypeStruct(shape, kind) fo...  1.41 us

profile of v3, /device:TPU:1, one launch (start us, length us, event | category | flops | bytes accessed | tf_op | source)
XLA Modules:
  0.0 43.4 jit_solution(5854114824663897629)
XLA Ops:
  0.6 41.3 %shard_map.120 = (bf16[32,128,128]{2,1,0:T(8,128)(2,1)S(1)}, f32[5,16,128]{2,1,0:T(8,128)S(1)}, f32[72,16,128]{2,1,0:T(8,128)S(1)}, f32[72,16,128]{2,1,0:T(8,128)S(1)}) custom-call(bf16[32,73]{1,0:T(8,128)(2,1)} %bitcast.11, s32[1,32]{1,0:T(1,128)} %bitcast.12, f32[1,32]{1,0:T(1,128)} %bitcast.13, s32[1,128]{1,0:T(1,128)} %bitcast.14, f32[1,128]{1,0:T(1,128)} %bitcast.15, ...), custom_call_target="tpu_custom_call" | custom-call | tf_op jit(solution)/shard_map/pallas_call | solution.py:697
  41.9 1.4 %shard_map.121 = (bf16[32,128,128]{2,1,0:T(8,128)(2,1)}, f32[5,16,128]{2,1,0:T(8,128)}, f32[72,16,128]{2,1,0:T(8,128)}, f32[72,16,128]{2,1,0:T(8,128)}) custom-call(bf16[32,128,128]{2,1,0:T(8,128)(2,1)S(1)} %get-tuple-element.12.refs_0_, f32[5,16,128]{2,1,0:T(8,128)S(1)} %get-tuple-element.13.refs_1_, f32[72,16,128]{2,1,0:T(8,128)S(1)} %get-tuple-element.14.refs_2_, ...), custom_call_target="tpu_custom_call" | custom-call | tf_op jit(solution)/shard_map/pallas_call | solution.py:707

commit v4 on v3

--- a/solution.py
+++ b/solution.py
@@ -20,11 +20,16 @@
 CCOL = 8
 CELLS = CROW * CCOL
 PACK = 48
-LO_J = 2
-NUM_J = 9
 TILES = 72
 HALF = 36
 PIECE = 3
+OWNERS = 12
+
+
+def owner_rank(plane):
+    x, y = plane // 4, lax.rem(plane, 4)
+    return x != y, jnp.minimum(x * 3 + y - (y > x).astype(jnp.int32), OWNERS - 1)
+
 EMBED_TILES = 5
 DIRS = [(dy, dx) for dy in (-1, 0, 1) for dx in (-1, 0, 1) if (dy, dx) != (0, 0)]
 
@@ -114,29 +119,6 @@
     colmix_ref[pl.ds(32, 32), :] = lo
 
 
-def lift(embed_ref, cells_ref, rowmix_ref, colmix_ref, mid_ref, l3_ref):
-    cells = [cells_ref[LO_J + j] for j in range(NUM_J)]
-    wide = jnp.concatenate(cells, axis=-1)
-    wide = jnp.concatenate([wide, jnp.zeros((8, NUM_J * HID), F32)], axis=0).astype(BF)
-    mid = dot_t(colmix_ref[...], jnp.concatenate([wide, wide], axis=0))
-    mid_ref[...] = mid[0:WIDE]
-    mix = rowmix_ref[...]
-    for start in range(0, ROWS + 4, 12):
-        rows = []
-        for i in range(start, start + 12):
-            first = (i + 30) // 8 - 1 - LO_J
-            total = None
-            for m in range(4):
-                weight = mix[m : m + 1, i : i + 1]
-                term = weight * mid_ref[:, pl.ds((first + m) * HID, HID)]
-                total = term if total is None else total + term
-            rows.append(total.astype(BF))
-        lifted = dot(jnp.concatenate(rows, axis=0), embed_ref[...])
-        for n in range(12):
-            i = start + n
-            store_shifted(l3_ref, i // 2, i % 2, lifted[n * WIDE : (n + 1) * WIDE])
-
-
 def spread_own(cot_ref, c3_ref):
     def step(q, carry):
         for t in range(2):
@@ -221,7 +203,31 @@
     back_ref[16] = y[720 + WIDE : 720 + 2 * WIDE]
 
 
-def make_hidden(lat, l3_ref, w1_ref, h3_ref, slope_ref):
+def lift_and_hide(lat, embed_ref, cells_ref, rowmix_ref, colmix_ref, w1_ref, l3_ref, h3_ref, slope_ref):
+    hi, lo = colmix_ref[pl.ds(0, 32), :], colmix_ref[pl.ds(32, 32), :]
+    mixer = jnp.concatenate([hi, lo, hi], axis=0).T[0:WIDE]
+    mix = rowmix_ref[...]
+    step = 6
+
+    def lift(start):
+        rows = []
+        for i in range(start, start + step):
+            first = (i + 30) // 8 - 1
+            total = None
+            for m in range(4):
+                term = mix[m : m + 1, i : i + 1] * cells_ref[first + m]
+                total = term if total is None else total + term
+            rows.append(total)
+        wide = jnp.concatenate(rows, axis=-1)
+        wide = jnp.concatenate([wide, jnp.zeros((8, step * HID), F32)], axis=0)
+        hi, lo = halves(wide)
+        fine = dot(mixer, jnp.concatenate([hi, hi, lo], axis=0)).astype(BF)
+        fine = jnp.concatenate([fine[:, n * HID : (n + 1) * HID] for n in range(step)], axis=0)
+        lifted = dot(fine, embed_ref[...])
+        for n in range(step):
+            i = start + n
+            store_shifted(l3_ref, i // 2, i % 2, lifted[n * WIDE : (n + 1) * WIDE])
+
     def finish(pre_all, first, count):
         for p in range(count):
             for s in range(2):
@@ -239,9 +245,13 @@
                 slope_ref[first + p, :, pl.ds(s * HID, HID)] = slope
 
     waiting = None
+    lift(0)
+    lift(step)
     for first in range(0, 17, 3):
         count = min(3, 17 - first)
         pre_all = dot(four_rows(l3_ref, first, count, WIDE), w1_ref[...])
+        if 2 * first + 2 * step < ROWS + 4:
+            lift(2 * first + 2 * step)
         if waiting is not None:
             finish(*waiting)
         waiting = (pre_all, first, count)
@@ -259,33 +269,60 @@
     lax.fori_loop(0, 17, step, 0)
 
 
-def make_delta(back_ref, slope_ref, d3_ref):
-    def step(p, carry):
+def make_delta(back_ref, slope_ref, d3_ref, first, count):
+    for p in range(first, first + count):
         for s in range(2):
             lanes = pl.ds(s * HID, HID)
             store_shifted(d3_ref, p, s, back_ref[p, :, lanes] * slope_ref[p, :, lanes])
-        return carry
-
-    lax.fori_loop(0, 17, step, 0)
-
-
-def rows_from(ref, start, lanes):
-    q, odd = start // 2, start % 2
+
+
+def rows_from(ref, start, lanes, count=ROWS):
+    q, odd, half = start // 2, start % 2, count // 2
     if odd == 0:
-        return ref[pl.ds(q, 16), :, pl.ds(0, COLS), lanes].reshape(ROWS * COLS, -1)
-    parts = [ref[pl.ds(q, 16), 1, pl.ds(0, COLS), lanes], ref[pl.ds(q + 1, 16), 0, pl.ds(0, COLS), lanes]]
-    return jnp.stack(parts, axis=1).reshape(ROWS * COLS, -1)
-
-
-def weight_grad(v_ref, v_start, u_ref, u_start, out_ref):
-    centre = pl.ds(HID, HID)
-    left = jnp.concatenate([rows_from(v_ref, v_start + a, centre) for a in range(3)], axis=-1)
-    right = rows_from(u_ref, u_start, pl.ds(0, 3 * HID))
-    grad = dot_t(left, right)
+        return ref[pl.ds(q, half), :, pl.ds(0, COLS), lanes].reshape(count * COLS, -1)
+    parts = [
+        ref[pl.ds(q, half), 1, pl.ds(0, COLS), lanes],
+        ref[pl.ds(q + 1, half), 0, pl.ds(0, COLS), lanes],
+    ]
+    return jnp.stack(parts, axis=1).reshape(count * COLS, -1)
+
+
+def tap_products(v_ref, v_start, u_ref, u_start, count=ROWS):
+    turned = []
+    for n in range(v_start, v_start + count + 2):
+        turned.append(v_ref[n // 2, n % 2, pl.ds(0, COLS), pl.ds(HID, HID)].T)
+    left = [jnp.concatenate(turned[a : a + count], axis=1) for a in range(3)]
+    wide = dot(jnp.concatenate(left, axis=0), rows_from(u_ref, u_start, pl.ds(0, 2 * HID), count))
+    left = [jnp.concatenate(turned[a : a + count : 2], axis=1) for a in range(4)]
+    right = []
+    for n in (u_start, u_start + 1):
+        rows = u_ref[pl.ds(n // 2, count // 2), n % 2, pl.ds(0, COLS), pl.ds(2 * HID, HID)]
+        right.append(rows.reshape(count // 2 * COLS, HID))
+    last = dot(jnp.concatenate(left, axis=0), jnp.concatenate(right, axis=-1))
+    blocks = []
+    for a in range(3):
+        line = wide[a * HID : (a + 1) * HID]
+        third = last[a * HID : (a + 1) * HID, 0:HID] + last[(a + 1) * HID : (a + 2) * HID, HID : 2 * HID]
+        blocks.append([line[:, 0:HID], line[:, HID : 2 * HID], third])
+    return blocks
+
+
+def store_taps(blocks, out_ref):
     for a in range(3):
         for b in range(3):
-            block = grad[a * HID : (a + 1) * HID, (2 - b) * HID : (3 - b) * HID]
-            out_ref[pl.ds((a * 3 + b) * 8, 8)] = block.reshape(8, 16, HID).astype(BF)
+            out_ref[pl.ds((a * 3 + b) * 8, 8)] = blocks[a][2 - b].reshape(8, 16, HID).astype(BF)
+
+
+def weight_grad(v_ref, v_start, u_ref, u_start, out_ref):
+    store_taps(tap_products(v_ref, v_start, u_ref, u_start), out_ref)
+
+
+def delta_and_grad(back_ref, slope_ref, d3_ref, l3_ref, out_ref):
+    make_delta(back_ref, slope_ref, d3_ref, 0, 9)
+    one = tap_products(l3_ref, 1, d3_ref, 1, 16)
+    make_delta(back_ref, slope_ref, d3_ref, 9, 8)
+    two = tap_products(l3_ref, 17, d3_ref, 17, 16)
+    store_taps([[x + y for x, y in zip(*lines)] for lines in zip(one, two)], out_ref)
 
 
 def back_to_embed(first, count, d3_ref, w1t_ref, cot_ref, rowmix_ref, colmix_ref, down_ref):
@@ -337,6 +374,9 @@
         self.mate = (self.lat, self.lon + 1 - 2 * self.core)
         self.planes = [lax.rem(self.plane + d, 16) for d in range(1, 16)]
         self.plane_mates = [self.spot(q, self.z) for q in self.planes]
+        x, y = self.plane // 4, lax.rem(self.plane, 4)
+        self.x_mates = [self.spot(lax.rem(x + d, 4) * 4 + y, self.z) for d in range(1, 4)]
+        self.y_mates = [self.spot(x * 4 + lax.rem(y + d, 4), self.z) for d in range(1, 4)]
         self.z_mates = [self.spot(self.plane, lax.rem(self.z + d, 4)) for d in range(1, 4)]
         self.around = [(lax.rem(self.lat + dy + 8, 8), lax.rem(self.lon + dx + 16, 16)) for dy, dx in DIRS]
 
@@ -371,27 +411,30 @@
         self.part, self.paired, self.half, self.got = part, paired, half, got
         self.mine, self.other, self.final, self.twin = mine, other, final, twin
         pairs = [(sems.at[2 * n], sems.at[2 * n + 1]) for n in range(5)]
+        self.place = place
+        self.owner, rank = owner_rank(place.plane)
         self.keep = place.core * HALF
-        self.own = pl.ds(place.plane * PIECE, PIECE)
+        self.own = pl.ds(rank * PIECE, PIECE)
         away = part.at[pl.ds(HALF - self.keep, HALF)]
         self.pair = Exchange([remote(away, paired, pairs[0], place.mate)], paired, pairs[0])
-        self.scatter = Exchange(
-            [
-                remote(half.at[pl.ds(q * PIECE, PIECE)], got.at[n], pairs[1], t)
-                for n, (q, t) in enumerate(zip(place.planes, place.plane_mates))
-            ],
-            got,
-            pairs[1],
-        )
+        self.scatter_sems, self.gather_sems = pairs[1], pairs[3]
         self.column = Exchange(
             [remote(mine, other.at[n], pairs[2], t) for n, t in enumerate(place.z_mates)], other, pairs[2]
         )
-        self.gather = Exchange(
-            [remote(final.at[self.own], final.at[self.own], pairs[3], t) for t in place.plane_mates],
-            final.at[pl.ds(0, 15 * PIECE)],
-            pairs[3],
-        )
-        self.swap = Exchange([remote(final.at[pl.ds(0, HALF)], twin, pairs[4], place.mate)], twin, pairs[4])
+        self.swap = Exchange([remote(final, twin, pairs[4], place.mate)], twin, pairs[4])
+
+    def take(self, ref, count, sem):
+        span = ref.at[pl.ds(0, count * PIECE)]
+        pltpu.make_async_copy(span, span, sem).wait()
+
+    def take_others(self, ref, sem):
+        @pl.when(self.owner)
+        def _():
+            self.take(ref, OWNERS - 1, sem)
+
+        @pl.when(jnp.logical_not(self.owner))
+        def _():
+            self.take(ref, OWNERS, sem)
 
     def step_pair(self):
         self.pair.start()
@@ -399,34 +442,44 @@
     def step_scatter(self):
         self.pair.arrive()
         total = self.part[pl.ds(self.keep, HALF)].astype(F32) + self.paired[...].astype(F32)
-        self.half[pl.ds(0, HALF)] = total.astype(BF)
-        self.half[pl.ds(HALF, 16 * PIECE - HALF)] = jnp.zeros((16 * PIECE - HALF, 16, HID), BF)
-        self.scatter.start()
+        self.half[...] = total.astype(BF)
+        for n, (q, t) in enumerate(zip(self.place.planes, self.place.plane_mates)):
+            owner, rank = owner_rank(q)
+
+            @pl.when(owner)
+            def _():
+                piece = self.half.at[pl.ds(rank * PIECE, PIECE)]
+                remote(piece, self.got.at[pl.ds(n * PIECE, PIECE)], self.scatter_sems, t).start()
 
     def step_column(self):
-        self.scatter.arrive()
-        total = self.half[self.own].astype(F32)
-        for n in range(15):
-            total = total + self.got[n].astype(F32)
-        self.mine[...] = total.astype(BF)
-        self.column.start()
+        @pl.when(self.owner)
+        def _():
+            self.take(self.got, 15, self.scatter_sems[1])
+            total = self.half[self.own].astype(F32)
+            for n in range(15):
+                total = total + self.got[pl.ds(n * PIECE, PIECE)].astype(F32)
+            self.mine[...] = total.astype(BF)
+            self.column.start()
 
     def step_gather(self):
-        self.column.arrive()
-        total = self.mine[...].astype(F32)
-        for n in range(3):
-            total = total + self.other[n].astype(F32)
-        self.final[self.own] = total.astype(BF)
-        self.gather.start()
+        @pl.when(self.owner)
+        def _():
+            self.column.arrive()
+            total = self.mine[...].astype(F32)
+            for n in range(3):
+                total = total + self.other[n].astype(F32)
+            self.final[self.own] = total.astype(BF)
+            for t in self.place.plane_mates:
+                remote(self.final.at[self.own], self.final.at[self.own], self.gather_sems, t).start()
 
     def step_swap(self, full_ref, out_ref, sem, scale):
-        self.gather.arrive()
+        self.take_others(self.final, self.gather_sems[1])
         self.swap.start()
         self.outs = [
             pltpu.make_async_copy(full_ref.at[part], out_ref.at[part], sem.at[n])
             for n, part in enumerate((pl.ds(self.keep, HALF), pl.ds(HALF - self.keep, HALF)))
         ]
-        full_ref[pl.ds(self.keep, HALF)] = self.final[pl.ds(0, HALF)].astype(F32) * scale
+        full_ref[pl.ds(self.keep, HALF)] = self.final[...].astype(F32) * scale
         self.outs[0].start()
 
     def finish(self, full_ref, scale):
@@ -435,8 +488,15 @@
         self.outs[1].start()
 
     def drain(self):
-        for e in (self.pair, self.scatter, self.column, self.gather, self.swap):
-            e.sent()
+        self.pair.sent()
+        self.swap.sent()
+        self.take_others(self.half, self.scatter_sems[0])
+
+        @pl.when(self.owner)
+        def _():
+            self.column.sent()
+            self.take(self.got, 15, self.gather_sems[0])
+
         for out in self.outs:
             out.wait()
 
@@ -448,7 +508,7 @@
         self.away = pl.ds(2 - place.core * 2, 3)
         self.steps = []
         base = 0
-        for g, targets in enumerate([[place.mate], place.z_mates, place.plane_mates, [place.mate]]):
+        for g, targets in enumerate([[place.mate], place.z_mates, place.x_mates, place.y_mates, [place.mate]]):
             size = EMBED_TILES if g == 0 else 3
             pair = (sems.at[2 * g], sems.at[2 * g + 1])
             copies = []
@@ -472,10 +532,10 @@
         self.steps[g + 1][2].start()
 
     def finish(self, out_ref, scale):
-        base, _, exchange = self.steps[3]
+        base, _, exchange = self.steps[4]
         exchange.arrive()
         out_ref[self.away] = self.slots[base, pl.ds(0, 3)].astype(F32) * scale
-        out_ref[self.keep] = self.parts[3, pl.ds(0, 3)].astype(F32) * scale
+        out_ref[self.keep] = self.parts[4, pl.ds(0, 3)].astype(F32) * scale
         for _, _, exchange in self.steps:
             exchange.sent()
 
@@ -501,7 +561,7 @@
     feat_ref, gemb_ref, g1_ref, g2_ref, out_sem,
     coarse_ref, row_src_ref, row_frac_ref, col_src_ref, col_frac_ref, embed_in_ref, conv1_ref, conv2_ref, cot_ref,
     lines_ref, pack_ref, embed_ref,
-    nb_ref, rowhalo_ref, colpack_ref, colhalo_ref, cells_ref, rowmix_ref, colmix_ref, mid_ref, down_ref,
+    nb_ref, rowhalo_ref, colpack_ref, colhalo_ref, cells_ref, rowmix_ref, colmix_ref, down_ref,
     w1_ref, w2_ref, w1t_ref, w2t_ref, l3_ref, c3_ref, h3_ref, d3_ref, back_ref, slope_ref,
     part1, paired1, half1, got1, mine1, other1, final1, twin1,
     part2, paired2, half2, got2, mine2, other2, final2, twin2, eparts, eslots,
@@ -552,14 +612,14 @@
     corners = Exchange(corners, colhalo_ref.at[:, pl.ds(4, 2)], pairs[3])
     sum1 = GradSum(place, part1, paired1, half1, got1, mine1, other1, final1, twin1, sum_sem.at[pl.ds(0, 10)])
     sum2 = GradSum(place, part2, paired2, half2, got2, mine2, other2, final2, twin2, sum_sem.at[pl.ds(10, 10)])
-    small = SmallSum(place, eparts, eslots, sum_sem.at[pl.ds(20, 8)])
+    small = SmallSum(place, eparts, eslots, sum_sem.at[pl.ds(20, 10)])
 
     for load in loads[0:5]:
         load.wait()
     pack_block(coarse_ref, row_src_ref, row_frac_ref, col_src_ref, col_frac_ref, lines_ref, pack_ref)
-    loads[5].wait()
     pl.semaphore_wait(barrier, len(partners))
     packs.start()
+    loads[5].wait()
     gather_columns(cot_ref, colpack_ref)
     columns.start()
 
@@ -580,8 +640,7 @@
     corners.start()
     rows.start()
     coarse_setup(lat, lon, nb_ref, cells_ref, rowmix_ref, colmix_ref)
-    lift(embed_ref, cells_ref, rowmix_ref, colmix_ref, mid_ref, l3_ref)
-    apart(make_hidden, lat, l3_ref, w1_ref, h3_ref, slope_ref)
+    apart(lift_and_hide, lat, embed_ref, cells_ref, rowmix_ref, colmix_ref, w1_ref, l3_ref, h3_ref, slope_ref)
     columns.arrive()
     close_columns(cot_ref, colhalo_ref, c3_ref)
     apart(weight_grad, h3_ref, 0, c3_ref, 2, part2)
@@ -591,36 +650,36 @@
     close_rows(lat, rowhalo_ref, colhalo_ref, c3_ref)
     apart(back_around, c3_ref, w2t_ref, back_ref)
     sum2.step_scatter()
-    make_delta(back_ref, slope_ref, d3_ref)
-    apart(weight_grad, l3_ref, 1, d3_ref, 1, part1)
+    apart(delta_and_grad, back_ref, slope_ref, d3_ref, l3_ref, part1)
     sum1.step_pair()
     apart(back_to_embed, 0, 8, d3_ref, w1t_ref, cot_ref, rowmix_ref, colmix_ref, down_ref)
     sum1.step_scatter()
     apart(back_to_embed, 8, 8, d3_ref, w1t_ref, cot_ref, rowmix_ref, colmix_ref, down_ref)
     embed_grad(cells_ref, down_ref, eparts.at[0])
     small.begin()
-    sum2.step_column()
     shift_hidden(h3_ref)
-    small.pass_on(0)
     done = [
         pltpu.make_async_copy(feat_ref.at[pl.ds(n * 16, 16)], feat_out.at[pl.ds(n * 16, 16)], out_sem.at[n])
         for n in range(2)
     ]
+    small.pass_on(0)
     apart(features_of, 0, 8, h3_ref, l3_ref, w2_ref, feat_ref)
     done[0].start()
+    sum2.step_column()
     apart(features_of, 8, 8, h3_ref, l3_ref, w2_ref, feat_ref)
     done[1].start()
-    sum2.step_gather()
     sum1.step_column()
     small.pass_on(1)
+    sum2.step_gather()
     sum1.step_gather()
+    small.pass_on(2)
     sum2.step_swap(g2_ref, g2_out, out_sem.at[pl.ds(2, 2)], scale)
-    small.pass_on(2)
+    small.pass_on(3)
+    sum1.step_swap(g1_ref, g1_out, out_sem.at[pl.ds(5, 2)], scale)
     sum2.finish(g2_ref, scale)
     small.finish(gemb_ref, scale)
     done.append(pltpu.make_async_copy(gemb_ref, gemb_out, out_sem.at[4]))
     done[2].start()
-    sum1.step_swap(g1_ref, g1_out, out_sem.at[pl.ds(5, 2)], scale)
     sum1.finish(g1_ref, scale)
     for exchange in (packs, columns, rows, corners):
         exchange.sent()
@@ -631,8 +690,7 @@
 
 
 def write_out(*refs):
-    count = (len(refs) - 1) // 2
-    copies = [pltpu.make_async_copy(refs[n], refs[count + n], refs[-1].at[n]) for n in range(count)]
+    copies = [pltpu.make_async_copy(refs[n], refs[n + 4], refs[-1].at[n]) for n in range(4)]
     for copy in copies:
         copy.start()
     for copy in copies:
@@ -652,8 +710,8 @@
     line = lambda n, kind: pltpu.VMEM((1, n), kind)
     tiles = lambda *n: pltpu.VMEM((*n, 16, HID), BF)
     grad = [
-        tiles(TILES), tiles(HALF), tiles(16 * PIECE), tiles(15, PIECE),
-        tiles(PIECE), tiles(3, PIECE), tiles(16 * PIECE), tiles(HALF),
+        tiles(TILES), tiles(HALF), tiles(HALF), tiles(15 * PIECE),
+        tiles(PIECE), tiles(3, PIECE), tiles(HALF), tiles(HALF),
     ]
     return (
         [pltpu.VMEM(shape, kind) for shape, kind in RESULTS]
@@ -675,7 +733,6 @@
             pltpu.VMEM((12, 24, HID), F32),
             pltpu.VMEM((8, HID), F32),
             pltpu.VMEM((64, 2 * HID), BF),
-            pltpu.VMEM((WIDE, NUM_J * HID), F32),
             pltpu.VMEM((12, 32, HID), F32),
         ]
         + [pltpu.VMEM((12 * HID, 2 * HID), BF)] * 4
@@ -684,9 +741,9 @@
         + [pltpu.VMEM((17, WIDE, 2 * HID), F32)] * 2
         + grad
         + grad
-        + [tiles(4, EMBED_TILES), tiles(20, EMBED_TILES)]
+        + [tiles(5, EMBED_TILES), tiles(11, EMBED_TILES)]
         + [dma((9,))]
-        + [dma((8,)), dma((28,))]
+        + [dma((8,)), dma((30,))]
     )
 
 

time: 43.5 us -> 42 us (0.966)
  Pallas kernels: 42.7 us -> 41.2 us
    pallas_call x1, Pallas kernels: 41.3 us -> 39.8 us  [on_device(): pl.pallas_call(kernel, out_shape=[pltpu.VMEM(shape, kind) for shape, kind...]
where the time goes in v4:
time: 42 us; the launch traced here: 41.9 us
  Pallas kernels  41.2 us (98%)
  between operations  0.64 us (2%)
    pallas_call x1, Pallas kernels, on_device(): pl.pallas_call(kernel, out_shape=[pltpu.VMEM(shape, kind) for shape, kind...  39.8 us
    pallas_call x1, Pallas kernels, on_device(): pl.pallas_call(write_out, out_shape=[jax.ShapeDtypeStruct(shape, kind) fo...  1.41 us

profile of v4, /device:TPU:1, one launch (start us, length us, event | category | flops | bytes accessed | tf_op | source)
XLA Modules:
  0.0 41.9 jit_solution(9360107632501684568)
XLA Ops:
  0.6 39.8 %shard_map.120 = (bf16[32,128,128]{2,1,0:T(8,128)(2,1)S(1)}, f32[5,16,128]{2,1,0:T(8,128)S(1)}, f32[72,16,128]{2,1,0:T(8,128)S(1)}, f32[72,16,128]{2,1,0:T(8,128)S(1)}) custom-call(bf16[32,73]{1,0:T(8,128)(2,1)} %bitcast.11, s32[1,32]{1,0:T(1,128)} %bitcast.12, f32[1,32]{1,0:T(1,128)} %bitcast.13, s32[1,128]{1,0:T(1,128)} %bitcast.14, f32[1,128]{1,0:T(1,128)} %bitcast.15, ...), custom_call_target="tpu_custom_call" | custom-call | tf_op jit(solution)/shard_map/pallas_call | solution.py:754
  40.5 1.4 %shard_map.121 = (bf16[32,128,128]{2,1,0:T(8,128)(2,1)}, f32[5,16,128]{2,1,0:T(8,128)}, f32[72,16,128]{2,1,0:T(8,128)}, f32[72,16,128]{2,1,0:T(8,128)}) custom-call(bf16[32,128,128]{2,1,0:T(8,128)(2,1)S(1)} %get-tuple-element.12.refs_0_, f32[5,16,128]{2,1,0:T(8,128)S(1)} %get-tuple-element.13.refs_1_, f32[72,16,128]{2,1,0:T(8,128)S(1)} %get-tuple-element.14.refs_2_, ...), custom_call_target="tpu_custom_call" | custom-call | tf_op jit(solution)/shard_map/pallas_call | solution.py:764

commit v5 on v4

--- a/solution.py
+++ b/solution.py
@@ -189,18 +189,18 @@
     back_ref[pl.ds(1, 15), pl.ds(16, 96), :] = y.reshape(15, 96, 2 * HID)
 
 
-def back_around(c3_ref, w2t_ref, back_ref):
-    parts = [
-        four_rows(c3_ref, 1, 15, 16, 0),
-        four_rows(c3_ref, 1, 15, 32, COLS - 16),
-        four_rows(c3_ref, 0, 1, WIDE),
-        four_rows(c3_ref, 16, 1, WIDE),
-    ]
+def back_beside(c3_ref, w2t_ref, back_ref):
+    parts = [four_rows(c3_ref, 1, 15, 16, 0), four_rows(c3_ref, 1, 15, 32, COLS - 16)]
     y = dot(jnp.concatenate(parts, axis=0), w2t_ref[...])
     back_ref[pl.ds(1, 15), pl.ds(0, 16), :] = y[0:240].reshape(15, 16, 2 * HID)
     back_ref[pl.ds(1, 15), pl.ds(COLS - 16, 32), :] = y[240:720].reshape(15, 32, 2 * HID)
-    back_ref[0] = y[720 : 720 + WIDE]
-    back_ref[16] = y[720 + WIDE : 720 + 2 * WIDE]
+
+
+def back_ends(c3_ref, w2t_ref, back_ref):
+    parts = [four_rows(c3_ref, 0, 1, WIDE), four_rows(c3_ref, 16, 1, WIDE)]
+    y = dot(jnp.concatenate(parts, axis=0), w2t_ref[...])
+    back_ref[0] = y[0:WIDE]
+    back_ref[16] = y[WIDE : 2 * WIDE]
 
 
 def lift_and_hide(lat, embed_ref, cells_ref, rowmix_ref, colmix_ref, w1_ref, l3_ref, h3_ref, slope_ref):
@@ -287,18 +287,28 @@
     return jnp.stack(parts, axis=1).reshape(count * COLS, -1)
 
 
-def tap_products(v_ref, v_start, u_ref, u_start, count=ROWS):
-    turned = []
-    for n in range(v_start, v_start + count + 2):
-        turned.append(v_ref[n // 2, n % 2, pl.ds(0, COLS), pl.ds(HID, HID)].T)
-    left = [jnp.concatenate(turned[a : a + count], axis=1) for a in range(3)]
-    wide = dot(jnp.concatenate(left, axis=0), rows_from(u_ref, u_start, pl.ds(0, 2 * HID), count))
-    left = [jnp.concatenate(turned[a : a + count : 2], axis=1) for a in range(4)]
-    right = []
-    for n in (u_start, u_start + 1):
-        rows = u_ref[pl.ds(n // 2, count // 2), n % 2, pl.ds(0, COLS), pl.ds(2 * HID, HID)]
-        right.append(rows.reshape(count // 2 * COLS, HID))
-    last = dot(jnp.concatenate(left, axis=0), jnp.concatenate(right, axis=-1))
+def tap_products(v_ref, u_ref, runs):
+    left, right = [[], [], []], []
+    left_two, right_two = [[], [], [], []], [[], []]
+    for v_start, u_start, count in runs:
+        turned = []
+        for n in range(v_start, v_start + count + 2):
+            turned.append(v_ref[n // 2, n % 2, pl.ds(0, COLS), pl.ds(HID, HID)].T)
+        for a in range(3):
+            left[a] += turned[a : a + count]
+        for a in range(4):
+            left_two[a] += turned[a : a + count : 2]
+        right.append(rows_from(u_ref, u_start, pl.ds(0, 2 * HID), count))
+        for s in range(2):
+            n = u_start + s
+            rows = u_ref[pl.ds(n // 2, count // 2), n % 2, pl.ds(0, COLS), pl.ds(2 * HID, HID)]
+            right_two[s].append(rows.reshape(count // 2 * COLS, HID))
+
+    def stack(lines):
+        return jnp.concatenate([jnp.concatenate(line, axis=1) for line in lines], axis=0)
+
+    wide = dot(stack(left), jnp.concatenate(right, axis=0))
+    last = dot(stack(left_two), jnp.concatenate([jnp.concatenate(x, axis=0) for x in right_two], axis=-1))
     blocks = []
     for a in range(3):
         line = wide[a * HID : (a + 1) * HID]
@@ -314,15 +324,23 @@
 
 
 def weight_grad(v_ref, v_start, u_ref, u_start, out_ref):
-    store_taps(tap_products(v_ref, v_start, u_ref, u_start), out_ref)
-
-
-def delta_and_grad(back_ref, slope_ref, d3_ref, l3_ref, out_ref):
-    make_delta(back_ref, slope_ref, d3_ref, 0, 9)
-    one = tap_products(l3_ref, 1, d3_ref, 1, 16)
-    make_delta(back_ref, slope_ref, d3_ref, 9, 8)
-    two = tap_products(l3_ref, 17, d3_ref, 17, 16)
-    store_taps([[x + y for x, y in zip(*lines)] for lines in zip(one, two)], out_ref)
+    store_taps(tap_products(v_ref, u_ref, [(v_start, u_start, ROWS)]), out_ref)
+
+
+def delta_inside(back_ref, slope_ref, d3_ref, l3_ref, held_ref):
+    make_delta(back_ref, slope_ref, d3_ref, 1, 9)
+    blocks = tap_products(l3_ref, d3_ref, [(3, 3, 16)])
+    make_delta(back_ref, slope_ref, d3_ref, 10, 6)
+    for a in range(3):
+        for n in range(3):
+            held_ref[a, n] = blocks[a][n]
+
+
+def delta_ends(back_ref, slope_ref, d3_ref, l3_ref, held_ref, out_ref):
+    make_delta(back_ref, slope_ref, d3_ref, 0, 1)
+    make_delta(back_ref, slope_ref, d3_ref, 16, 1)
+    blocks = tap_products(l3_ref, d3_ref, [(1, 1, 2), (19, 19, 14)])
+    store_taps([[blocks[a][n] + held_ref[a, n] for n in range(3)] for a in range(3)], out_ref)
 
 
 def back_to_embed(first, count, d3_ref, w1t_ref, cot_ref, rowmix_ref, colmix_ref, down_ref):
@@ -562,7 +580,7 @@
     coarse_ref, row_src_ref, row_frac_ref, col_src_ref, col_frac_ref, embed_in_ref, conv1_ref, conv2_ref, cot_ref,
     lines_ref, pack_ref, embed_ref,
     nb_ref, rowhalo_ref, colpack_ref, colhalo_ref, cells_ref, rowmix_ref, colmix_ref, down_ref,
-    w1_ref, w2_ref, w1t_ref, w2t_ref, l3_ref, c3_ref, h3_ref, d3_ref, back_ref, slope_ref,
+    w1_ref, w2_ref, w1t_ref, w2t_ref, l3_ref, c3_ref, h3_ref, d3_ref, back_ref, slope_ref, held_ref,
     part1, paired1, half1, got1, mine1, other1, final1, twin1,
     part2, paired2, half2, got2, mine2, other2, final2, twin2, eparts, eslots,
     load_sem, halo_sem, sum_sem,
@@ -636,21 +654,23 @@
     embed_ref[pl.ds(0, embed_in_ref.shape[0]), :] = embed_in_ref[...]
     down_ref[...] = jnp.zeros_like(down_ref)
 
+    columns.arrive()
+    close_columns(cot_ref, colhalo_ref, c3_ref)
+    apart(back_beside, c3_ref, w2t_ref, back_ref)
     packs.arrive()
     corners.start()
     rows.start()
     coarse_setup(lat, lon, nb_ref, cells_ref, rowmix_ref, colmix_ref)
     apart(lift_and_hide, lat, embed_ref, cells_ref, rowmix_ref, colmix_ref, w1_ref, l3_ref, h3_ref, slope_ref)
-    columns.arrive()
-    close_columns(cot_ref, colhalo_ref, c3_ref)
     apart(weight_grad, h3_ref, 0, c3_ref, 2, part2)
     sum2.step_pair()
+    apart(delta_inside, back_ref, slope_ref, d3_ref, l3_ref, held_ref)
+    sum2.step_scatter()
     corners.arrive()
     rows.arrive()
     close_rows(lat, rowhalo_ref, colhalo_ref, c3_ref)
-    apart(back_around, c3_ref, w2t_ref, back_ref)
-    sum2.step_scatter()
-    apart(delta_and_grad, back_ref, slope_ref, d3_ref, l3_ref, part1)
+    apart(back_ends, c3_ref, w2t_ref, back_ref)
+    apart(delta_ends, back_ref, slope_ref, d3_ref, l3_ref, held_ref, part1)
     sum1.step_pair()
     apart(back_to_embed, 0, 8, d3_ref, w1t_ref, cot_ref, rowmix_ref, colmix_ref, down_ref)
     sum1.step_scatter()
@@ -739,6 +759,7 @@
         + [pltpu.VMEM((18, 2, WIDE, 3 * HID), BF)] * 2
         + [pltpu.VMEM((17, 2, WIDE, 3 * HID), BF)] * 2
         + [pltpu.VMEM((17, WIDE, 2 * HID), F32)] * 2
+        + [pltpu.VMEM((3, 3, HID, HID), F32)]
         + grad
         + grad
         + [tiles(5, EMBED_TILES), tiles(11, EMBED_TILES)]

time: 42 us -> 41.9 us (level)
  no operation moved by 1% of the time
where the time goes in v5:
time: 41.9 us; the launch traced here: 41.8 us
  Pallas kernels  41.1 us (98%)
  between operations  0.64 us (2%)
    pallas_call x1, Pallas kernels, on_device(): pl.pallas_call(kernel, out_shape=[pltpu.VMEM(shape, kind) for shape, kind...  39.7 us
    pallas_call x1, Pallas kernels, on_device(): pl.pallas_call(write_out, out_shape=[jax.ShapeDtypeStruct(shape, kind) fo...  1.41 us

profile of v5, /device:TPU:1, one launch (start us, length us, event | category | flops | bytes accessed | tf_op | source)
XLA Modules:
  0.0 41.8 jit_solution(4523004750815674047)
XLA Ops:
  0.6 39.7 %shard_map.120 = (bf16[32,128,128]{2,1,0:T(8,128)(2,1)S(1)}, f32[5,16,128]{2,1,0:T(8,128)S(1)}, f32[72,16,128]{2,1,0:T(8,128)S(1)}, f32[72,16,128]{2,1,0:T(8,128)S(1)}) custom-call(bf16[32,73]{1,0:T(8,128)(2,1)} %bitcast.11, s32[1,32]{1,0:T(1,128)} %bitcast.12, f32[1,32]{1,0:T(1,128)} %bitcast.13, s32[1,128]{1,0:T(1,128)} %bitcast.14, f32[1,128]{1,0:T(1,128)} %bitcast.15, ...), custom_call_target="tpu_custom_call" | custom-call | tf_op jit(solution)/shard_map/pallas_call | solution.py:775
  40.4 1.4 %shard_map.121 = (bf16[32,128,128]{2,1,0:T(8,128)(2,1)}, f32[5,16,128]{2,1,0:T(8,128)}, f32[72,16,128]{2,1,0:T(8,128)}, f32[72,16,128]{2,1,0:T(8,128)}) custom-call(bf16[32,128,128]{2,1,0:T(8,128)(2,1)S(1)} %get-tuple-element.12.refs_0_, f32[5,16,128]{2,1,0:T(8,128)S(1)} %get-tuple-element.13.refs_1_, f32[72,16,128]{2,1,0:T(8,128)S(1)} %get-tuple-element.14.refs_2_, ...), custom_call_target="tpu_custom_call" | custom-call | tf_op jit(solution)/shard_map/pallas_call | solution.py:785

commit v6 on v5

--- a/solution.py
+++ b/solution.py
@@ -31,7 +31,9 @@
     return x != y, jnp.minimum(x * 3 + y - (y > x).astype(jnp.int32), OWNERS - 1)
 
 EMBED_TILES = 5
-DIRS = [(dy, dx) for dy in (-1, 0, 1) for dx in (-1, 0, 1) if (dy, dx) != (0, 0)]
+DIRS = [(-1, -1), (-1, 1), (1, -1), (1, 1), (-1, 0), (1, 0), (0, -1), (0, 1)]
+FAR_FIRST = [(d // 4, d % 4) for d in range(1, 16)]
+FAR_FIRST.sort(key=lambda s: -min(s[0], 4 - s[0]) - min(s[1], 4 - s[1]))
 
 
 def dot(a, b):
@@ -390,9 +392,9 @@
         self.z = lax.rem(self.lat, 2) * 2 + lax.rem(self.lon // 2, 2)
         self.plane = self.lon // 4 * 4 + self.lat // 2
         self.mate = (self.lat, self.lon + 1 - 2 * self.core)
-        self.planes = [lax.rem(self.plane + d, 16) for d in range(1, 16)]
+        x, y = self.plane // 4, lax.rem(self.plane, 4)
+        self.planes = [lax.rem(x + a, 4) * 4 + lax.rem(y + b, 4) for a, b in FAR_FIRST]
         self.plane_mates = [self.spot(q, self.z) for q in self.planes]
-        x, y = self.plane // 4, lax.rem(self.plane, 4)
         self.x_mates = [self.spot(lax.rem(x + d, 4) * 4 + y, self.z) for d in range(1, 4)]
         self.y_mates = [self.spot(x * 4 + lax.rem(y + d, 4), self.z) for d in range(1, 4)]
         self.z_mates = [self.spot(self.plane, lax.rem(self.z + d, 4)) for d in range(1, 4)]

time: 41.9 us -> 41.8 us (level)
  no operation moved by 1% of the time
where the time goes in v6:
time: 41.8 us; the launch traced here: 41.7 us
  Pallas kernels  41 us (98%)
  between operations  0.64 us (2%)
    pallas_call x1, Pallas kernels, on_device(): pl.pallas_call(kernel, out_shape=[pltpu.VMEM(shape, kind) for shape, kind...  39.6 us
    pallas_call x1, Pallas kernels, on_device(): pl.pallas_call(write_out, out_shape=[jax.ShapeDtypeStruct(shape, kind) fo...  1.41 us

profile of v6, /device:TPU:1, one launch (start us, length us, event | category | flops | bytes accessed | tf_op | source)
XLA Modules:
  0.0 41.7 jit_solution(9959586785273543140)
XLA Ops:
  0.6 39.6 %shard_map.120 = (bf16[32,128,128]{2,1,0:T(8,128)(2,1)S(1)}, f32[5,16,128]{2,1,0:T(8,128)S(1)}, f32[72,16,128]{2,1,0:T(8,128)S(1)}, f32[72,16,128]{2,1,0:T(8,128)S(1)}) custom-call(bf16[32,73]{1,0:T(8,128)(2,1)} %bitcast.11, s32[1,32]{1,0:T(1,128)} %bitcast.12, f32[1,32]{1,0:T(1,128)} %bitcast.13, s32[1,128]{1,0:T(1,128)} %bitcast.14, f32[1,128]{1,0:T(1,128)} %bitcast.15, ...), custom_call_target="tpu_custom_call" | custom-call | tf_op jit(solution)/shard_map/pallas_call | solution.py:777
  40.3 1.4 %shard_map.121 = (bf16[32,128,128]{2,1,0:T(8,128)(2,1)}, f32[5,16,128]{2,1,0:T(8,128)}, f32[72,16,128]{2,1,0:T(8,128)}, f32[72,16,128]{2,1,0:T(8,128)}) custom-call(bf16[32,128,128]{2,1,0:T(8,128)(2,1)S(1)} %get-tuple-element.12.refs_0_, f32[5,16,128]{2,1,0:T(8,128)S(1)} %get-tuple-element.13.refs_1_, f32[72,16,128]{2,1,0:T(8,128)S(1)} %get-tuple-element.14.refs_2_, ...), custom_call_target="tpu_custom_call" | custom-call | tf_op jit(solution)/shard_map/pallas_call | solution.py:787
